TPU v7x, 128 devices: a whole 4x4x4 slice. The times are simulated.
128 devices in a mesh: ta: 16 (over y_hi, x, core), ha: 8 (over z, y_lo).
Axes of the slice: x: 4, y: 4 (y_hi: 2, y_lo: 2; y = y_hi * 2 + y_lo), z: 4, core: 2. Of those that a mesh axis runs over, the one named last changes fastest.
Arguments:
- query_seq: bfloat16 [32768, 1536], P(('ta', 'ha')), may hold values from -6 to 6
- key_seq: bfloat16 [32768, 1536], P(('ta', 'ha')), may hold values from -6 to 6
- value_seq: bfloat16 [32768, 1536], P(('ta', 'ha')), may hold values from -6 to 6
- tile_order: int32 [32768], replicated, may hold values from 0 to 32767, as said below
- grad_output: bfloat16 [64, 64, 8, 1536], P('ta', 'ha'), may hold values from -6 to 6
Outputs:
- attended: bfloat16 [64, 64, 8, 1536], P('ta', 'ha')
- grad_query: bfloat16 [64, 64, 8, 1536], P('ta', 'ha')
- grad_key: bfloat16 [64, 64, 8, 1536], P('ta', 'ha')
- grad_value: bfloat16 [64, 64, 8, 1536], P('ta', 'ha')
Inputs may be any that keep to these rules, and one draw needn't show every extreme that they name: `tile_order`: A permutation of the raster indices; every aligned run of 256 sequence positions holds exactly 2 tokens of each aligned block of 4 frames by 8 rows.
All inputs are finite; a program needn't handle non-finite values.
Results may differ from a plain program's by a relative error of at most 0.0082.
Values may be sent and summed in bfloat16 or wider, within the bound.
A program may use at most 192 MiB of HBM per device.

v0:
```python
import jax
import jax.numpy as jnp
from jax import lax
from jax.sharding import PartitionSpec as P

HEADS = 12
HEAD_DIM = 128
TILE_FRAMES = 4
TILE_ROWS = 8
TILE_COLS = 8


score_floor = -1e30


def from_behind(block, axis, distance):
    devices = range(lax.axis_size(axis))
    route = [(i - distance, i) for i in devices if i - distance in devices]
    return lax.ppermute(block, axis, route)


def with_halo(array, sides, width):
    for axis, dim in sides:
        count, length = (lax.axis_size(axis), array.shape[dim])
        up = [(i, (i + 1) % count) for i in range(count - 1)]
        down = [(j, i) for i, j in up]
        last = lax.slice_in_dim(array, length - width, length, axis=dim)
        initial = lax.slice_in_dim(array, 0, width, axis=dim)
        before = lax.ppermute(last, axis, up)
        after = lax.ppermute(initial, axis, down)
        array = jnp.concatenate([before, array, after], axis=dim)
    return array


def window_usable(
    frame_first, row_first, total_frames, total_rows, block_frames, block_rows, grid_cols
):
    query_frames = jnp.arange(block_frames) // TILE_FRAMES
    query_rows = jnp.arange(block_rows) // TILE_ROWS
    key_frames = jnp.arange(block_frames + 2 * TILE_FRAMES)
    key_rows = jnp.arange(block_rows + 2 * TILE_ROWS)
    frame_global = frame_first + key_frames - TILE_FRAMES
    row_global = row_first + key_rows - TILE_ROWS
    near_frames = jnp.abs(query_frames[:, None] - (key_frames[None, :] // TILE_FRAMES - 1)) <= 1
    near_frames = near_frames & ((frame_global >= 0) & (frame_global < total_frames))[None, :]
    near_rows = jnp.abs(query_rows[:, None] - (key_rows[None, :] // TILE_ROWS - 1)) <= 1
    near_rows = near_rows & ((row_global >= 0) & (row_global < total_rows))[None, :]
    col_tiles = jnp.arange(grid_cols) // TILE_COLS
    near_cols = jnp.abs(col_tiles[:, None] - col_tiles[None, :]) <= 1
    usable = (
        near_frames[:, None, None, :, None, None]
        & near_rows[None, :, None, None, :, None]
        & near_cols[None, None, :, None, None, :]
    )
    ext_frames = block_frames + 2 * TILE_FRAMES
    ext_rows = block_rows + 2 * TILE_ROWS
    return usable.reshape(block_frames * block_rows * grid_cols, ext_frames * ext_rows * grid_cols)


def head_pass(query_head, key_head, value_head, grad_head, usable):
    score_scale = HEAD_DIM ** (-0.5)
    scores = jnp.dot(query_head, key_head.T, preferred_element_type=jnp.float32) * score_scale
    scores = jnp.where(usable, scores, score_floor)
    row_top = jnp.max(scores, axis=1, keepdims=True)
    weights = jnp.where(usable, jnp.exp(scores - row_top), 0.0)
    row_total = jnp.sum(weights, axis=1, keepdims=True)
    probabilities = weights / row_total
    probs_low = probabilities.astype(jnp.bfloat16)
    out_full = jnp.dot(probs_low, value_head, preferred_element_type=jnp.float32)
    grad_prob = jnp.dot(grad_head, value_head.T, preferred_element_type=jnp.float32)
    row_delta = jnp.sum(grad_head.astype(jnp.float32) * out_full, axis=1, keepdims=True)
    grad_score = (probabilities * (grad_prob - row_delta) * score_scale).astype(jnp.bfloat16)
    grad_query = jnp.dot(grad_score, key_head, preferred_element_type=jnp.float32).astype(
        jnp.bfloat16
    )
    grad_key = jnp.dot(grad_score.T, query_head, preferred_element_type=jnp.float32)
    grad_value = jnp.dot(probs_low.T, grad_head, preferred_element_type=jnp.float32)
    return (out_full.astype(jnp.bfloat16), grad_query, grad_key, grad_value)


def split_heads(matrix):
    return matrix.reshape(matrix.shape[0], HEADS, HEAD_DIM).transpose(1, 0, 2)


def join_heads(stacked):
    return stacked.transpose(1, 0, 2).reshape(stacked.shape[1], HEADS * HEAD_DIM)


def all_heads(query_rows, key_ext, value_ext, grad_rows, usable):

    def one_head(head_parts):
        return head_pass(head_parts[0], head_parts[1], head_parts[2], head_parts[3], usable)

    results = lax.map(
        one_head,
        (
            split_heads(query_rows),
            split_heads(key_ext),
            split_heads(value_ext),
            split_heads(grad_rows),
        ),
    )
    return tuple((join_heads(member) for member in results))


def source_range(step_value, tile_size, block_size):
    if step_value < 0:
        return (0, tile_size)
    if step_value > 0:
        return (tile_size + block_size, 2 * tile_size + block_size)
    return (tile_size, tile_size + block_size)


def send_back(sent_piece, offset):
    return from_behind(sent_piece, ("ta", "ha"), offset)


def shards(query_seq, key_seq, value_seq, tile_order, grad_output):
    block_frames, block_rows, grid_cols, channel_count = grad_output.shape
    tok_rows = query_seq.shape[0]
    frame_parts = lax.axis_size("ta")
    row_parts = lax.axis_size("ha")
    frame_index = lax.axis_index("ta")
    row_index = lax.axis_index("ha")
    total_frames = block_frames * frame_parts
    total_rows = block_rows * row_parts
    own_slots = lax.dynamic_slice_in_dim(
        tile_order, (frame_index * row_parts + row_index) * tok_rows, tok_rows
    )
    frame_of = own_slots // (total_rows * grid_cols)
    row_of = own_slots // grid_cols % total_rows
    target = frame_of // block_frames * row_parts + row_of // block_rows
    send_order = jnp.argsort(target, stable=True)
    outgoing = (query_seq[send_order], key_seq[send_order], value_seq[send_order])
    arrived = (
        lax.all_to_all(outgoing[0], ("ta", "ha"), split_axis=0, concat_axis=0, tiled=True),
        lax.all_to_all(outgoing[1], ("ta", "ha"), split_axis=0, concat_axis=0, tiled=True),
        lax.all_to_all(outgoing[2], ("ta", "ha"), split_axis=0, concat_axis=0, tiled=True),
    )
    first_frame = frame_index * block_frames
    first_row = row_index * block_rows
    raster = (
        (first_frame + jnp.arange(block_frames))[:, None, None] * total_rows
        + (first_row + jnp.arange(block_rows))[None, :, None]
    ) * grid_cols + jnp.arange(grid_cols)[None, None, :]
    slot_table = (
        jnp.zeros(tile_order.shape, jnp.int32)
        .at[tile_order]
        .set(jnp.arange(tile_order.shape[0], dtype=jnp.int32))
    )
    source_slots = slot_table[raster.reshape(-1)]
    arrival_rank = jnp.argsort(jnp.argsort(source_slots))
    query_tile = arrived[0][arrival_rank]
    key_tile = arrived[1][arrival_rank]
    value_tile = arrived[2][arrival_rank]
    block_shape = (block_frames, block_rows, grid_cols, channel_count)
    kv_pair = jnp.stack((key_tile.reshape(block_shape), value_tile.reshape(block_shape)), axis=3)
    ext_frames = block_frames + 2 * TILE_FRAMES
    ext_rows = block_rows + 2 * TILE_ROWS
    tile_view = kv_pair.reshape(
        block_frames // TILE_FRAMES,
        TILE_FRAMES,
        block_rows // TILE_ROWS,
        TILE_ROWS,
        grid_cols,
        2,
        channel_count,
    )
    grown_view = with_halo(tile_view, (("ta", 0), ("ha", 2)), 1)
    extended = grown_view.reshape(ext_frames, ext_rows, grid_cols, 2, channel_count)
    ext_count = ext_frames * ext_rows * grid_cols
    key_ext = extended[:, :, :, 0].reshape(ext_count, channel_count)
    value_ext = extended[:, :, :, 1].reshape(ext_count, channel_count)
    usable = window_usable(
        first_frame, first_row, total_frames, total_rows, block_frames, block_rows, grid_cols
    )
    grad_rows = grad_output.reshape(tok_rows, channel_count)
    attended, grad_query, grad_key_ext, grad_value_ext = all_heads(
        query_tile, key_ext, value_ext, grad_rows, usable
    )
    ext_shape = (ext_frames, ext_rows, grid_cols, channel_count)
    grad_pair = jnp.stack(
        (grad_key_ext.reshape(ext_shape), grad_value_ext.reshape(ext_shape)), axis=3
    )
    own_block = grad_pair[
        TILE_FRAMES : TILE_FRAMES + block_frames, TILE_ROWS : TILE_ROWS + block_rows
    ]
    for frame_step in (-1, 0, 1):
        for row_step in (-1, 0, 1):
            if frame_step == 0 and row_step == 0:
                continue
            frame_low, frame_high = source_range(frame_step, TILE_FRAMES, block_frames)
            row_low, row_high = source_range(row_step, TILE_ROWS, block_rows)
            sent_piece = grad_pair[frame_low:frame_high, row_low:row_high].astype(jnp.bfloat16)
            arrived_piece = send_back(sent_piece, frame_step * row_parts + row_step).astype(
                jnp.float32
            )
            own_block = own_block + arrived_piece
    grad_key = own_block[:, :, :, 0].astype(jnp.bfloat16)
    grad_value = own_block[:, :, :, 1].astype(jnp.bfloat16)
    return (attended.reshape(block_shape), grad_query.reshape(block_shape), grad_key, grad_value)


def solution(mesh):
    in_specs = (
        P(("ta", "ha"), None),
        P(("ta", "ha"), None),
        P(("ta", "ha"), None),
        P(),
        P("ta", "ha", None, None),
    )
    out_specs = (
        P("ta", "ha", None, None),
        P("ta", "ha", None, None),
        P("ta", "ha", None, None),
        P("ta", "ha", None, None),
    )
    return jax.shard_map(shards, mesh=mesh, in_specs=in_specs, out_specs=out_specs, check_vma=False)
```

profile of v0, /device:TPU:4, one launch (start us, length us, event | category | flops | bytes accessed | tf_op | source)
XLA Modules:
  0.0 1347.5 jit_solution(18272587911028690734)
XLA Ops:
  39.1 120.1 %scatter_custom_fusion = s32[32768]{0:T(1024)S(1)} fusion(s32[32768]{0:T(1024)S(1)} %compare_select_fusion, s32[32768]{0:T(1024)S(1)} %iota.62, s32[]{:T(128)} %copy.53), kind=kCustom, calls=%fused_computation.69 | custom fusion | bytes 131076 | tf_op jit(solution)/shard_map/scatter | solution.py:149
  177.1 15.8 %collective-permute-done.1 = bf16[1,4,1,8,8,2,1536]{6,4,5,3,2,1,0:T(8,128)(2,1)S(1)} collective-permute-done((bf16[1,4,1,8,8,2,1536]{6,4,5,3,2,1,0:T(8,128)(2,1)S(1)}, bf16[1,4,1,8,8,2,1536]{6,4,5,3,2,1,0:T(8,128)(2,1)S(1)}, u32[]{:S(2)}, u32[]{:S(2)}) %collective-permute-start.1) | collective-permute-done | bytes 1572896 | tf_op jit(solution)/shard_map/ppermute | solution.py:30
  226.5 192.6 %all-to-all-done = bf16[128,2,1536]{2,1,0:T(2,128)(2,1)} async-done(((bf16[128,2,1536]{2,1,0:T(2,128)(2,1)}), bf16[128,2,1536]{2,1,0:T(2,128)(2,1)}, u32[]{:S(2)}, u32[]{:S(2)}) %all-to-all-start) | async-done | bytes 786464 | tf_op jit(solution)/shard_map/all_to_all | solution.py:136
  478.9 544.5 %while.17 = (s32[]{:T(128)}, bf16[12,256,128]{1,2,0:T(8,128)(2,1)S(1)}, bf16[12,256,128]{2,1,0:T(8,128)(2,1)}, f32[12,2304,128]{2,1,0:T(8,128)}, f32[12,2304,128...) while((s32[]{:T(128)}, ...), condition=%wide.region_8.9_spmd.clone, body=%wide.region_4.8_spmd.clone.sunk | while | flops 915569920 | bytes 29055168 | solution.py:94
  485.1 24.8 %and.244 = pred[256,2304]{1,0:T(32,128)(4,1)S(1)} reshape(pred[4,8,8,12,24,8]{5,4,3,2,1,0:T(8,128)(4,1)} %broadcast_and_fusion.3) | data formatting | bytes 1179648 | tf_op jit(solution)/shard_map/and | solution.py:51
  530.5 24.8 %and.244 = pred[256,2304]{1,0:T(32,128)(4,1)S(1)} reshape(pred[4,8,8,12,24,8]{5,4,3,2,1,0:T(8,128)(4,1)} %broadcast_and_fusion.3) | data formatting | bytes 1179648 | tf_op jit(solution)/shard_map/and | solution.py:51
  575.9 24.8 %and.244 = pred[256,2304]{1,0:T(32,128)(4,1)S(1)} reshape(pred[4,8,8,12,24,8]{5,4,3,2,1,0:T(8,128)(4,1)} %broadcast_and_fusion.3) | data formatting | bytes 1179648 | tf_op jit(solution)/shard_map/and | solution.py:51
  621.2 24.8 %and.244 = pred[256,2304]{1,0:T(32,128)(4,1)S(1)} reshape(pred[4,8,8,12,24,8]{5,4,3,2,1,0:T(8,128)(4,1)} %broadcast_and_fusion.3) | data formatting | bytes 1179648 | tf_op jit(solution)/shard_map/and | solution.py:51
  666.6 24.8 %and.244 = pred[256,2304]{1,0:T(32,128)(4,1)S(1)} reshape(pred[4,8,8,12,24,8]{5,4,3,2,1,0:T(8,128)(4,1)} %broadcast_and_fusion.3) | data formatting | bytes 1179648 | tf_op jit(solution)/shard_map/and | solution.py:51
  711.9 24.8 %and.244 = pred[256,2304]{1,0:T(32,128)(4,1)S(1)} reshape(pred[4,8,8,12,24,8]{5,4,3,2,1,0:T(8,128)(4,1)} %broadcast_and_fusion.3) | data formatting | bytes 1179648 | tf_op jit(solution)/shard_map/and | solution.py:51
  757.3 24.8 %and.244 = pred[256,2304]{1,0:T(32,128)(4,1)S(1)} reshape(pred[4,8,8,12,24,8]{5,4,3,2,1,0:T(8,128)(4,1)} %broadcast_and_fusion.3) | data formatting | bytes 1179648 | tf_op jit(solution)/shard_map/and | solution.py:51
  802.6 24.8 %and.244 = pred[256,2304]{1,0:T(32,128)(4,1)S(1)} reshape(pred[4,8,8,12,24,8]{5,4,3,2,1,0:T(8,128)(4,1)} %broadcast_and_fusion.3) | data formatting | bytes 1179648 | tf_op jit(solution)/shard_map/and | solution.py:51
  848.0 24.8 %and.244 = pred[256,2304]{1,0:T(32,128)(4,1)S(1)} reshape(pred[4,8,8,12,24,8]{5,4,3,2,1,0:T(8,128)(4,1)} %broadcast_and_fusion.3) | data formatting | bytes 1179648 | tf_op jit(solution)/shard_map/and | solution.py:51
  893.4 24.8 %and.244 = pred[256,2304]{1,0:T(32,128)(4,1)S(1)} reshape(pred[4,8,8,12,24,8]{5,4,3,2,1,0:T(8,128)(4,1)} %broadcast_and_fusion.3) | data formatting | bytes 1179648 | tf_op jit(solution)/shard_map/and | solution.py:51
  938.8 24.8 %and.244 = pred[256,2304]{1,0:T(32,128)(4,1)S(1)} reshape(pred[4,8,8,12,24,8]{5,4,3,2,1,0:T(8,128)(4,1)} %broadcast_and_fusion.3) | data formatting | bytes 1179648 | tf_op jit(solution)/shard_map/and | solution.py:51
  984.1 24.8 %and.244 = pred[256,2304]{1,0:T(32,128)(4,1)S(1)} reshape(pred[4,8,8,12,24,8]{5,4,3,2,1,0:T(8,128)(4,1)} %broadcast_and_fusion.3) | data formatting | bytes 1179648 | tf_op jit(solution)/shard_map/and | solution.py:51
  1023.5 17.6 %copy.27 = f32[2304,12,128]{2,1,0:T(8,128)} copy(f32[2304,12,128]{2,0,1:T(8,128)} %bitcast.115) | data formatting | bytes 28311552 | tf_op jit(solution)/shard_map/transpose | solution.py:86
  1041.0 17.7 %stack_reshape_reshape.7 = f32[12,24,8,1,1536]{4,2,1,0,3:T(8,128)} reshape(f32[2304,12,128]{2,1,0:T(8,128)} %copy.27) | data formatting | bytes 28311552 | tf_op jit(solution)/shard_map/stack;reshape;reshape | solution.py:182
  1058.7 17.5 %copy.26 = f32[2304,12,128]{2,1,0:T(8,128)} copy(f32[2304,12,128]{2,0,1:T(8,128)} %bitcast.116) | data formatting | bytes 28311552 | tf_op jit(solution)/shard_map/transpose | solution.py:86
  1076.2 17.7 %stack_reshape_reshape.6 = f32[12,24,8,1,1536]{4,2,1,0,3:T(8,128)} reshape(f32[2304,12,128]{2,1,0:T(8,128)} %copy.26) | data formatting | bytes 28311552 | tf_op jit(solution)/shard_map/stack;reshape;reshape | solution.py:182
  1145.8 72.4 %collective-permute-done.4 = bf16[4,8,8,2,1536]{4,2,1,0,3:T(8,128)(2,1)S(1)} collective-permute-done((bf16[4,8,8,2,1536]{4,2,1,0,3:T(8,128)(2,1)S(1)}, bf16[4,8,8,2,1536]{4,2,1,0,3:T(8,128)(2,1)S(1)}, u32[]{:S(2)}, u32[]{:S(2)}) %collective-permute-start.4) | collective-permute-done | bytes 1572896 | tf_op jit(solution)/shard_map/ppermute | solution.py:19
  1218.2 36.4 %collective-permute-start.7 = (bf16[4,8,8,2,1536]{4,2,1,0,3:T(8,128)(2,1)}, bf16[4,8,8,2,1536]{4,2,1,0,3:T(8,128)(2,1)}, u32[]{:S(2)}, u32[]{:S(2)}) collective-permute-start(bf16[4,8,8,2,1536]{4,2,1,0,3:T(8,128)(2,1)} %get-tuple-element.148), channel_id=1, source_target_pairs={{1,0},{2,1},{3,2},{4,3},{5,4},{6,5},{7,6},{8,7},{9,8},{10,9},{11,1... | collective-permute-start | bytes 4718600 | tf_op jit(solution)/shard_map/ppermute | solution.py:19
  1263.9 55.4 %collective-permute-done.8 = bf16[4,8,8,2,1536]{4,2,1,0,3:T(8,128)(2,1)} collective-permute-done((bf16[4,8,8,2,1536]{4,2,1,0,3:T(8,128)(2,1)}, bf16[4,8,8,2,1536]{4,2,1,0,3:T(8,128)(2,1)}, u32[]{:S(2)}, u32[]{:S(2)}) %collective-permute-start.8) | collective-permute-done | bytes 1572896 | tf_op jit(solution)/shard_map/ppermute | solution.py:19
  1319.3 18.8 %collective-permute-done.7 = bf16[4,8,8,2,1536]{4,2,1,0,3:T(8,128)(2,1)} collective-permute-done((bf16[4,8,8,2,1536]{4,2,1,0,3:T(8,128)(2,1)}, bf16[4,8,8,2,1536]{4,2,1,0,3:T(8,128)(2,1)}, u32[]{:S(2)}, u32[]{:S(2)}) %collective-permute-start.7) | collective-permute-done | bytes 1572896 | tf_op jit(solution)/shard_map/ppermute | solution.py:19
  (237 shorter events, 465.6 us)
Async XLA Ops:
  6.3 11.7 copy-start.2
  7.4 25.8 %all-to-all-start.2 = ((bf16[128,2,1536]{2,1,0:T(2,128)(2,1)}), bf16[128,2,1536]{2,1,0:T(2,128)(2,1)S(1)}, u32[]{:S(2)}, u32[]{:S(2)}) async-start(bf16[128,2,1536]{2,1,0:T(2,128)(2,1)} %all_to_all.30), calls=%async_computation.2 | async-start | bytes 1572864 | tf_op jit(solution)/shard_map/all_to_all | solution.py:138
  19.2 19.8 %copy-start.12 = (s32[32768]{0:T(1024)S(1)}, s32[32768]{0:T(1024)}, u32[]{:S(2)}) copy-start(s32[32768]{0:T(1024)} %param.10) | copy-start | bytes 393220
  33.2 135.6 %all-to-all-start.1 = ((bf16[128,2,1536]{2,1,0:T(2,128)(2,1)}), bf16[128,2,1536]{2,1,0:T(2,128)(2,1)S(1)}, u32[]{:S(2)}, u32[]{:S(2)}) async-start(bf16[128,2,1536]{2,1,0:T(2,128)(2,1)} %all_to_all.27), calls=%async_computation.1 | async-start | bytes 1572864 | tf_op jit(solution)/shard_map/all_to_all | solution.py:137
  172.6 34.9 %copy-start.3 = (bf16[256,1536]{1,0:T(8,128)(2,1)S(1)}, bf16[256,1536]{1,0:T(8,128)(2,1)}, u32[]{:S(2)}) copy-start(bf16[256,1536]{1,0:T(8,128)(2,1)} %param.7) | copy-start | bytes 2359300
  172.6 20.3 %collective-permute-start.1 = (bf16[1,4,1,8,8,2,1536]{6,4,5,3,2,1,0:T(8,128)(2,1)S(1)}, bf16[1,4,1,8,8,2,1536]{6,4,5,3,2,1,0:T(8,128)(2,1)S(1)}, u32[]{:S(2)}, u32[]{:S(2)}) collective-permute-start(bf16[1,4,1,8,8,2,1536]{6,4,5,3,2,1,0:T(8,128)(2,1)S(1)} %maximum_bitcast_fusion), channel_id=1, source_target_pairs={{8,0},{16,8},{24,16},{32,24},{40,32},{48,40},{56,48},{64,56},{72,6... | collective-permute-start | bytes 4718600 | tf_op jit(solution)/shard_map/ppermute | solution.py:30
  175.0 21.7 %collective-permute-start = (bf16[1,4,1,8,8,2,1536]{6,4,5,3,2,1,0:T(8,128)(2,1)S(1)}, bf16[1,4,1,8,8,2,1536]{6,4,5,3,2,1,0:T(8,128)(2,1)S(1)}, u32[]{:S(2)}, u32[]{:S(2)}) collective-permute-start(bf16[1,4,1,8,8,2,1536]{6,4,5,3,2,1,0:T(8,128)(2,1)S(1)} %maximum_bitcast_fusion), channel_id=1, source_target_pairs={{0,8},{8,16},{16,24},{24,32},{32,40},{40,48},{48,56},{56,64},{64,7... | collective-permute-start | bytes 4718600 | tf_op jit(solution)/shard_map/ppermute | solution.py:29
  192.9 6.5 copy-start.4
  199.4 224.4 %collective-permute-start.3 = (bf16[3,4,1,8,8,2,1536]{6,4,5,3,2,1,0:T(8,128)(2,1)}, bf16[3,4,1,8,8,2,1536]{6,4,5,3,2,1,0:T(8,128)(2,1)}, u32[]{:S(2)}, u32[]{:S(2)}) collective-permute-start(bf16[3,4,1,8,8,2,1536]{6,4,5,3,2,1,0:T(8,128)(2,1)} %pad_maximum_fusion.1), channel_id=1, source_target_pairs={{1,0},{2,1},{3,2},{4,3},{5,4},{6,5},{7,6},{9,8},{10,9},{11,10},{12... | collective-permute-start | bytes 14155784 | tf_op jit(solution)/shard_map/ppermute | solution.py:30
  200.7 223.1 %collective-permute-start.2 = (bf16[3,4,1,8,8,2,1536]{6,4,5,3,2,1,0:T(8,128)(2,1)}, bf16[3,4,1,8,8,2,1536]{6,4,5,3,2,1,0:T(8,128)(2,1)}, u32[]{:S(2)}, u32[]{:S(2)}) collective-permute-start(bf16[3,4,1,8,8,2,1536]{6,4,5,3,2,1,0:T(8,128)(2,1)} %pad_maximum_fusion.1), channel_id=1, source_target_pairs={{0,1},{1,2},{2,3},{3,4},{4,5},{5,6},{6,7},{8,9},{9,10},{10,11},{11... | collective-permute-start | bytes 14155784 | tf_op jit(solution)/shard_map/ppermute | solution.py:29
  208.7 15.3 %copy-start.8 = (bf16[4,8,8,1536]{3,2,1,0:T(8,128)(2,1)S(1)}, bf16[4,8,8,1536]{3,2,1,0:T(8,128)(2,1)}, u32[]{:S(2)}) copy-start(bf16[4,8,8,1536]{3,2,1,0:T(8,128)(2,1)} %param.11) | copy-start | bytes 2359300
  209.9 209.2 %all-to-all-start = ((bf16[128,2,1536]{2,1,0:T(2,128)(2,1)}), bf16[128,2,1536]{2,1,0:T(2,128)(2,1)}, u32[]{:S(2)}, u32[]{:S(2)}) async-start(bf16[128,2,1536]{2,1,0:T(2,128)(2,1)} %all_to_all.24), calls=%async_computation | async-start | bytes 1572864 | tf_op jit(solution)/shard_map/all_to_all | solution.py:136
  470.5 8.5 copy-start.10
  1023.5 17.6 %copy-start.11 = (bf16[12,256,128]{1,2,0:T(8,128)(2,1)}, bf16[12,256,128]{1,2,0:T(8,128)(2,1)S(1)}, u32[]{:S(2)}) copy-start(bf16[12,256,128]{1,2,0:T(8,128)(2,1)S(1)} %get-tuple-element.65) | copy-start | bytes 2359300
  1130.8 131.2 %copy-start.9 = (bf16[12,256,128]{2,1,0:T(8,128)(2,1)S(1)}, bf16[12,256,128]{2,1,0:T(8,128)(2,1)}, u32[]{:S(2)}) copy-start(bf16[12,256,128]{2,1,0:T(8,128)(2,1)} %get-tuple-element.66) | copy-start | bytes 2359300
  1130.8 87.3 %collective-permute-start.4 = (bf16[4,8,8,2,1536]{4,2,1,0,3:T(8,128)(2,1)S(1)}, bf16[4,8,8,2,1536]{4,2,1,0,3:T(8,128)(2,1)S(1)}, u32[]{:S(2)}, u32[]{:S(2)}) collective-permute-start(bf16[4,8,8,2,1536]{4,2,1,0,3:T(8,128)(2,1)S(1)} %get-tuple-element.143), channel_id=1, source_target_pairs={{9,0},{10,1},{11,2},{12,3},{13,4},{14,5},{15,6},{16,7},{17,8},{18,... | collective-permute-start | bytes 4718600 | tf_op jit(solution)/shard_map/ppermute | solution.py:19
  1133.0 121.5 %collective-permute-start.11 = (bf16[4,8,8,2,1536]{4,2,1,0,3:T(8,128)(2,1)S(1)}, bf16[4,8,8,2,1536]{4,2,1,0,3:T(8,128)(2,1)S(1)}, u32[]{:S(2)}, u32[]{:S(2)}) collective-permute-start(bf16[4,8,8,2,1536]{4,2,1,0,3:T(8,128)(2,1)S(1)} %get-tuple-element.144), channel_id=1, source_target_pairs={{0,9},{1,10},{2,11},{3,12},{4,13},{5,14},{6,15},{7,16},{8,17},{9,1... | collective-permute-start | bytes 4718600 | tf_op jit(solution)/shard_map/ppermute | solution.py:19
  1136.5 119.9 %collective-permute-start.10 = (bf16[4,8,8,2,1536]{4,2,1,0,3:T(8,128)(2,1)S(1)}, bf16[4,8,8,2,1536]{4,2,1,0,3:T(8,128)(2,1)S(1)}, u32[]{:S(2)}, u32[]{:S(2)}) collective-permute-start(bf16[4,8,8,2,1536]{4,2,1,0,3:T(8,128)(2,1)S(1)} %get-tuple-element.145), channel_id=1, source_target_pairs={{0,8},{1,9},{2,10},{3,11},{4,12},{5,13},{6,14},{7,15},{8,16},{9,17... | collective-permute-start | bytes 4718600 | tf_op jit(solution)/shard_map/ppermute | solution.py:19
  1140.0 123.9 %collective-permute-start.9 = (bf16[4,8,8,2,1536]{4,2,1,0,3:T(8,128)(2,1)}, bf16[4,8,8,2,1536]{4,2,1,0,3:T(8,128)(2,1)}, u32[]{:S(2)}, u32[]{:S(2)}) collective-permute-start(bf16[4,8,8,2,1536]{4,2,1,0,3:T(8,128)(2,1)} %get-tuple-element.146), channel_id=1, source_target_pairs={{0,7},{1,8},{2,9},{3,10},{4,11},{5,12},{6,13},{7,14},{8,15},{9,16}... | collective-permute-start | bytes 4718600 | tf_op jit(solution)/shard_map/ppermute | solution.py:19
  1143.9 175.5 %collective-permute-start.8 = (bf16[4,8,8,2,1536]{4,2,1,0,3:T(8,128)(2,1)}, bf16[4,8,8,2,1536]{4,2,1,0,3:T(8,128)(2,1)}, u32[]{:S(2)}, u32[]{:S(2)}) collective-permute-start(bf16[4,8,8,2,1536]{4,2,1,0,3:T(8,128)(2,1)} %get-tuple-element.147), channel_id=1, source_target_pairs={{0,1},{1,2},{2,3},{3,4},{4,5},{5,6},{6,7},{7,8},{8,9},{9,10},{10,1... | collective-permute-start | bytes 4718600 | tf_op jit(solution)/shard_map/ppermute | solution.py:19
  1218.2 120.0 %collective-permute-start.7 = (bf16[4,8,8,2,1536]{4,2,1,0,3:T(8,128)(2,1)}, bf16[4,8,8,2,1536]{4,2,1,0,3:T(8,128)(2,1)}, u32[]{:S(2)}, u32[]{:S(2)}) collective-permute-start(bf16[4,8,8,2,1536]{4,2,1,0,3:T(8,128)(2,1)} %get-tuple-element.148), channel_id=1, source_target_pairs={{1,0},{2,1},{3,2},{4,3},{5,4},{6,5},{7,6},{8,7},{9,8},{10,9},{11,1... | collective-permute-start | bytes 4718600 | tf_op jit(solution)/shard_map/ppermute | solution.py:19
  1254.5 84.2 %collective-permute-start.6 = (bf16[4,8,8,2,1536]{4,2,1,0,3:T(8,128)(2,1)}, bf16[4,8,8,2,1536]{4,2,1,0,3:T(8,128)(2,1)}, u32[]{:S(2)}, u32[]{:S(2)}) collective-permute-start(bf16[4,8,8,2,1536]{4,2,1,0,3:T(8,128)(2,1)} %get-tuple-element.149), channel_id=1, source_target_pairs={{7,0},{8,1},{9,2},{10,3},{11,4},{12,5},{13,6},{14,7},{15,8},{16,9}... | collective-permute-start | bytes 4718600 | tf_op jit(solution)/shard_map/ppermute | solution.py:19
  1256.5 82.2 %collective-permute-start.5 = (bf16[4,8,8,2,1536]{4,2,1,0,3:T(8,128)(2,1)}, bf16[4,8,8,2,1536]{4,2,1,0,3:T(8,128)(2,1)}, u32[]{:S(2)}, u32[]{:S(2)}) collective-permute-start(bf16[4,8,8,2,1536]{4,2,1,0,3:T(8,128)(2,1)} %get-tuple-element.150), channel_id=1, source_target_pairs={{8,0},{9,1},{10,2},{11,3},{12,4},{13,5},{14,6},{15,7},{16,8},{17,9... | collective-permute-start | bytes 4718600 | tf_op jit(solution)/shard_map/ppermute | solution.py:19
  1338.7 8.6 copy-start.1
  (4 other events, 12.9 us)
where the time goes:
time: 1360 us; the launch traced here: 1350 us
  local copies, waits for them, and re-layouts  591 us (43%)
  waiting for transfers between devices  372 us (27%)
  matrix products  145 us (11%)
  other arithmetic  139 us (10%)
  starting transfers between devices  98 us (7%)
    and x12, local copies, waits for them, and re-layouts, window_usable(): near_frames[:, None, None, :, None, None]  298 us
    all_to_all x1, waiting for transfers between devices, shards(): lax.all_to_all(outgoing[0], ('ta', 'ha'), split_axis=0, concat_axis=0, ti...  193 us
    ppermute x8, waiting for transfers between devices, from_behind(): return lax.ppermute(block, axis, route)  147 us
    scatter x1, local copies, waits for them, and re-layouts, shards(): slot_table = jnp.zeros(tile_order.shape, jnp.int32).at[tile_order].set(jn...  120 us
    and x13, other arithmetic, window_usable(): near_frames[:, None, None, :, None, None]  71.9 us
    ppermute x8, starting transfers between devices, from_behind(): return lax.ppermute(block, axis, route)  55.1 us
    another operation x3, local copies, waits for them, and re-layouts, shards(): jnp.stack((grad_key_ext.reshape(ext_shape), grad_value_ext.reshape(ext_sh...  47 us
    transpose x4, local copies, waits for them, and re-layouts, join_heads(): stacked.transpose(1, 0, 2).reshape(stacked.shape[1], HEADS * HEAD_DIM)  37.8 us
  transfers between devices with their start and end apart: 15, of which 8 were waited for; matrix products, arithmetic and copies ran while one was open for 11% of the time, Pallas kernels for 0%

commit v1 on v0

v1 whole, which is shorter than its diff:
```python
import functools

import jax
import jax.numpy as jnp
from jax import lax
from jax.experimental import pallas as pl
from jax.experimental.pallas import tpu as pltpu
from jax.sharding import PartitionSpec as P

HEADS = 12
HEAD_DIM = 128
GROUP_HEADS = 3
TILE_FRAMES = 4
TILE_ROWS = 8
SCALE = HEAD_DIM ** (-0.5)
LOG2E = 1.4426950408889634
NEG = -1e30
MESH = pl.DeviceIdType.MESH
F32 = jnp.float32
BF16 = jnp.bfloat16
DIRECTIONS = [(a, b) for a in (-1, 0, 1) for b in (-1, 0, 1) if (a, b) != (0, 0)]


def dot(a, b):
    return jnp.dot(a, b, preferred_element_type=F32)


def dot_nt(a, b):
    return lax.dot_general(a, b, (((1,), (1,)), ((), ())), preferred_element_type=F32)


def iota(shape, dim):
    return lax.broadcasted_iota(jnp.int32, shape, dim)


def own_part(step):
    return {1: 2, -1: 1, 0: pl.ds(1, 2)}[step]


def halo_part(step):
    return {1: 3, -1: 0, 0: pl.ds(1, 2)}[step]


def kernel(
    nt, nh, cols,
    q_ref, k_ref, v_ref, order_ref, grad_ref,
    att_ref, dq_ref, dk_ref, dv_ref,
    pair, sort_one, send, recv, place, ext, ext_t, query_t, grad_blocks, grad_t,
    score, prob, acc, own_acc, back_send, back_recv, stage,
    pair_sem, pair_send_sem, pair_recv_sem,
    grad_sem, grad_send_sem, grad_recv_sem,
    all_sem, all_send_sem, all_recv_sem,
    halo_send_sem, halo_recv_sem, back_send_sem, back_recv_sem,
    out_sem, out_send_sem, out_recv_sem,
):
    tok = TILE_FRAMES * TILE_ROWS * cols
    nk, nz = nt // 2, nh // 2
    chips = nk * nh
    width = GROUP_HEADS * HEAD_DIM
    ta, ha = lax.axis_index("ta"), lax.axis_index("ha")
    kk, core = ta // 2, ta % 2
    zz, half = ha // 2, ha % 2
    chip = kk * nh + ha
    others = [(1 - core, half), (core, 1 - half), (1 - core, 1 - half)]

    def mate(where):
        return (2 * kk + where[0], 2 * zz + where[1])

    def exists(dk, dz):
        okay = []
        if dk < 0:
            okay.append(kk > 0)
        if dk > 0:
            okay.append(kk < nk - 1)
        if dz < 0:
            okay.append(zz > 0)
        if dz > 0:
            okay.append(zz < nz - 1)
        return functools.reduce(jnp.logical_and, okay)

    for there, index in (
        (kk == 0, (0, slice(None))),
        (kk == nk - 1, (3, slice(None))),
        (zz == 0, (slice(None), 0)),
        (zz == nz - 1, (slice(None), 3)),
    ):

        @pl.when(there)
        def _():
            def clear(h, carry):
                for n in range(4):
                    at = tuple(n if isinstance(x, slice) else x for x in index)
                    ext[(h,) + at] = jnp.zeros((tok, 2 * HEAD_DIM), BF16)
                    back_recv[(h,) + at] = jnp.zeros((tok, 2 * HEAD_DIM), BF16)
                return carry

            lax.fori_loop(0, GROUP_HEADS, clear, 0)

    barrier = pltpu.get_barrier_semaphore()

    def greet(d, carry):
        to = lax.rem(chip + d, chips)
        pl.semaphore_signal(
            barrier, inc=1, device_id=(2 * (to // nh) + core, to % nh), device_id_type=MESH
        )
        return carry

    lax.fori_loop(1, chips, greet, 0)
    for where in ((1 - core, half), (1 - core, 1 - half)):
        pl.semaphore_signal(barrier, inc=1, device_id=mate(where), device_id_type=MESH)

    seq = (q_ref, k_ref, v_ref)
    pair_width = 2 * width
    own_cols = pl.ds(pl.multiple_of(core * pair_width, pair_width), pair_width)
    far_cols = pl.ds(pl.multiple_of((1 - core) * pair_width, pair_width), pair_width)
    own_rows = pl.ds(pl.multiple_of(core * tok, tok), tok)
    for a in range(3):
        pltpu.make_async_copy(
            seq[a].at[:, own_cols], pair.at[a, own_rows], pair_sem.at[a]
        ).start()

    def group_cols(where, n=width):
        return pl.ds(pl.multiple_of((2 * where[0] + where[1]) * width, width), width)

    own_block = 2 * core + half
    pltpu.make_async_copy(
        grad_ref.at[:, group_cols((core, half))], grad_blocks.at[own_block], grad_sem
    ).start()

    pl.semaphore_wait(barrier, chips + 1)

    def pair_copy(a):
        return pltpu.make_async_remote_copy(
            src_ref=seq[a].at[:, far_cols],
            dst_ref=pair.at[a, own_rows],
            send_sem=pair_send_sem.at[a],
            recv_sem=pair_recv_sem.at[a],
            device_id=mate((1 - core, half)),
            device_id_type=MESH,
        )

    def grad_copy(n):
        return pltpu.make_async_remote_copy(
            src_ref=grad_ref.at[:, group_cols(others[n])],
            dst_ref=grad_blocks.at[own_block],
            send_sem=grad_send_sem.at[n],
            recv_sem=grad_recv_sem.at[n],
            device_id=mate(others[n]),
            device_id_type=MESH,
        )

    for a in range(3):
        pair_copy(a).start()
    for n in range(3):
        grad_copy(n).start()

    def decode(t):
        frame = t // (nh * TILE_ROWS * cols)
        row = (t // cols) % (nh * TILE_ROWS)
        frame_block, row_block = frame // TILE_FRAMES, row // TILE_ROWS
        inside = ((frame % TILE_FRAMES) * TILE_ROWS + row % TILE_ROWS) * cols + t % cols
        return frame_block, row_block, inside

    order = order_ref[...]
    order_t = order.T
    for cc in range(2):
        source = kk * 2 * nh + cc * nh + ha
        line = order_ref[pl.ds(source, 1), :]
        column = jnp.sum(
            jnp.where(iota(order_t.shape, 1) == source, order_t, 0), axis=1, keepdims=True
        )
        line_f, line_r, _ = decode(line)
        col_f, col_r, _ = decode(column)
        same = (line_f * nh + line_r) == (col_f * nh + col_r)
        earlier = iota((tok, tok), 0) < iota((tok, tok), 1)
        second = jnp.sum(jnp.where(same & earlier, 1, 0), axis=0, keepdims=True)
        region = (line_f // 2) * nz + line_r // 2
        seat = region * 16 + ((line_f % 2) * 2 + line_r % 2) * 4 + cc * 2 + second
        sort_one[:, cc * tok : (cc + 1) * tok] = jnp.where(
            iota((2 * tok, tok), 0) == seat, 1.0, 0.0
        ).astype(BF16)

    for a in range(3):
        pltpu.make_async_copy(
            seq[a].at[:, own_cols], pair.at[a, own_rows], pair_sem.at[a]
        ).wait()
        pair_copy(a).wait_recv()

    def all_copy(h, d):
        to = lax.rem(chip + d, chips)
        to_k, to_h = to // nh, to % nh
        region = to_k * nz + to_h // 2
        return pltpu.make_async_remote_copy(
            src_ref=send.at[h, to_h % 2, pl.ds(pl.multiple_of(region * 16, 16), 16)],
            dst_ref=recv.at[h, pl.ds(pl.multiple_of(chip * 16, 16), 16)],
            send_sem=all_send_sem.at[h],
            recv_sem=all_recv_sem.at[h],
            device_id=(2 * to_k + core, to_h),
            device_id_type=MESH,
        )

    def all_own(h):
        region = kk * nz + zz
        return pltpu.make_async_copy(
            send.at[h, half, pl.ds(pl.multiple_of(region * 16, 16), 16)],
            recv.at[h, pl.ds(pl.multiple_of(chip * 16, 16), 16)],
            all_sem.at[h],
        )

    def send_head(h, carry):
        for a in range(3):
            left = pl.ds(pl.multiple_of(h * HEAD_DIM, HEAD_DIM), HEAD_DIM)
            right = pl.ds(pl.multiple_of(width + h * HEAD_DIM, HEAD_DIM), HEAD_DIM)
            both = jnp.concatenate([pair[a, :, left], pair[a, :, right]], axis=1)
            sorted_rows = dot(sort_one[...], both).astype(BF16)
            into = slice(a * HEAD_DIM, (a + 1) * HEAD_DIM)
            send[h, 0, :, into] = sorted_rows[:, :HEAD_DIM]
            send[h, 1, :, into] = sorted_rows[:, HEAD_DIM:]
        all_own(h).start()

        def push(d, inner):
            all_copy(h, d).start()
            return inner

        lax.fori_loop(1, chips, push, 0)
        return carry

    lax.fori_loop(0, GROUP_HEADS, send_head, 0)

    frame_block, row_block, inside = decode(order_t)
    block_of = frame_block * nh + row_block
    code = iota(order_t.shape, 0) * tok + inside
    found = []
    for b in range(4):
        mine = block_of == (2 * kk + b // 2) * nh + 2 * zz + b % 2
        found.append(jnp.min(jnp.where(mine, code, tok * tok), axis=0, keepdims=True) % tok)
        found.append(jnp.max(jnp.where(mine, code, 0), axis=0, keepdims=True) % tok)
    table = jnp.concatenate(found, axis=0).astype(F32).astype(BF16)
    rows = 4 * tok
    number = iota((nt * nh, rows), 1)
    from_chip, place_in = number // 16, number % 16
    sender = (from_chip // nh) * 2 * nh + ((place_in // 2) % 2) * nh + from_chip % nh
    spread = jnp.where(iota((nt * nh, rows), 0) == sender, 1.0, 0.0).astype(BF16)
    wide = dot(table, spread)
    lane = iota((8, rows), 1) % 16
    chosen = iota((8, rows), 0) == (lane // 4) * 2 + lane % 2
    position = jnp.sum(jnp.where(chosen, wide, 0.0), axis=0, keepdims=True).astype(jnp.int32)
    position = position + (iota((1, rows), 1) % 16 // 4) * tok

    def fill_place(b, carry):
        place[b] = jnp.where(iota((tok, rows), 0) + b * tok == position, 1.0, 0.0).astype(BF16)
        return carry

    lax.fori_loop(0, 4, fill_place, 0)

    pltpu.make_async_copy(
        grad_ref.at[:, group_cols((core, half))], grad_blocks.at[own_block], grad_sem
    ).wait()
    for n in range(3):
        grad_copy(n).wait_recv()

    def turn_grad(b, carry):
        for h in range(GROUP_HEADS):
            piece = grad_blocks[b, :, h * HEAD_DIM : (h + 1) * HEAD_DIM]
            grad_t[h, b] = piece.astype(F32).T.astype(BF16)
        return carry

    lax.fori_loop(0, 4, turn_grad, 0)

    def halo_copy(h, n):
        dk, dz = DIRECTIONS[n]
        return pltpu.make_async_remote_copy(
            src_ref=ext.at[h, own_part(dk), own_part(dz)],
            dst_ref=ext.at[h, halo_part(-dk), halo_part(-dz)],
            send_sem=halo_send_sem.at[h, n],
            recv_sem=halo_recv_sem.at[h, n],
            device_id=(ta + 2 * dk, ha + 2 * dz),
            device_id_type=MESH,
        )

    def back_copy(h, n):
        dk, dz = DIRECTIONS[n]
        return pltpu.make_async_remote_copy(
            src_ref=back_send.at[h, halo_part(dk), halo_part(dz)],
            dst_ref=back_recv.at[h, halo_part(-dk), halo_part(-dz)],
            send_sem=back_send_sem.at[h, n],
            recv_sem=back_recv_sem.at[h, n],
            device_id=(ta + 2 * dk, ha + 2 * dz),
            device_id_type=MESH,
        )

    def each_sent(step):
        for n, (dk, dz) in enumerate(DIRECTIONS):
            pl.when(exists(dk, dz))(functools.partial(step, n))

    def each_arrival(step):
        for n, (dk, dz) in enumerate(DIRECTIONS):
            pl.when(exists(-dk, -dz))(functools.partial(step, n))

    def settle(h, carry):
        all_own(h).wait()
        many = pl.ds(0, 16 * (chips - 1))
        pltpu.make_async_copy(recv.at[h, many], recv.at[h, many], all_recv_sem.at[h]).wait()

        def one_block(b, inner):
            grid_rows = dot(place[b], recv[h])
            query_t[h, b] = grid_rows[:, :HEAD_DIM].T.astype(BF16)
            ext[h, 1 + b // 2, 1 + b % 2] = grid_rows[:, HEAD_DIM:].astype(BF16)
            return inner

        lax.fori_loop(0, 4, one_block, 0)
        each_sent(lambda n: halo_copy(h, n).start())
        return carry

    lax.fori_loop(0, GROUP_HEADS, settle, 0)

    outs = (att_ref, dq_ref, dk_ref, dv_ref)

    def out_cols(h):
        first = ((2 * core + half) * GROUP_HEADS + h) * HEAD_DIM
        return pl.ds(pl.multiple_of(first, HEAD_DIM), HEAD_DIM)

    def out_copy(o, h, n):
        return pltpu.make_async_remote_copy(
            src_ref=stage.at[o, h, 2 * others[n][0] + others[n][1]],
            dst_ref=outs[o].at[:, out_cols(h)],
            send_sem=out_send_sem.at[o],
            recv_sem=out_recv_sem.at[o],
            device_id=mate(others[n]),
            device_id_type=MESH,
        )

    def out_own(o, h):
        return pltpu.make_async_copy(
            stage.at[o, h, own_block], outs[o].at[:, out_cols(h)], out_sem.at[o]
        )

    def hand_out(o, h):
        for n in range(3):
            out_copy(o, h, n).start()
        out_own(o, h).start()

    def attend(h, carry):
        each_arrival(lambda n: halo_copy(h, n).wait_recv())

        def prepare(e, inner):
            ext_t[e // 4, e % 4] = ext[h, e // 4, e % 4].astype(F32).T.astype(BF16)
            acc[e // 4, e % 4] = jnp.zeros((tok, 2 * HEAD_DIM), F32)
            return inner

        lax.fori_loop(0, 16, prepare, 0)

        def one_block(b, inner):
            bi, bj = b // 2, b % 2
            q_t, g_t = query_t[h, b], grad_t[h, b]
            spots = [(bi + di, bj + dj) for di in range(3) for dj in range(3)]
            biases = []
            for i, j in spots:
                missing = (
                    ((kk == 0) & (i == 0))
                    | ((kk == nk - 1) & (i == 3))
                    | ((zz == 0) & (j == 0))
                    | ((zz == nz - 1) & (j == 3))
                )
                biases.append(jnp.where(missing, NEG, 0.0).astype(F32))
            top = jnp.full((1, tok), NEG, F32)
            for n, (i, j) in enumerate(spots):
                s = dot(ext[h, i, j, :, :HEAD_DIM], q_t)
                score[n] = s
                top = jnp.maximum(top, jnp.max(s, axis=0, keepdims=True) + biases[n])
            shift = top * (SCALE * LOG2E)
            total = jnp.zeros((1, tok), F32)
            out_t = jnp.zeros((HEAD_DIM, tok), F32)
            for n, (i, j) in enumerate(spots):
                p = jnp.exp2(score[n] * (SCALE * LOG2E) - (shift - biases[n]))
                total = total + jnp.sum(p, axis=0, keepdims=True)
                p_low = p.astype(BF16)
                prob[n] = p_low
                out_t = out_t + dot(ext_t[i, j, HEAD_DIM:, :], p_low)
            inverse = 1.0 / total
            out_t = out_t * inverse
            grad_f = g_t.astype(F32)
            delta = jnp.sum(grad_f * out_t, axis=0, keepdims=True)
            stage[0, h, b] = out_t.T.astype(BF16)
            g_scaled = (grad_f * inverse).astype(BF16)
            q_scaled = (q_t.astype(F32) * (inverse * SCALE)).astype(BF16)
            dq_t = jnp.zeros((HEAD_DIM, tok), F32)
            for n, (i, j) in enumerate(spots):
                dp = dot(ext[h, i, j, :, HEAD_DIM:], g_t)
                p_low = prob[n]
                ds = (p_low.astype(F32) * (dp - delta)).astype(BF16)
                dq_t = dq_t + dot(ext_t[i, j, :HEAD_DIM, :], ds)
                acc[i, j, :, :HEAD_DIM] += dot_nt(ds, q_scaled)
                acc[i, j, :, HEAD_DIM:] += dot_nt(p_low, g_scaled)
            stage[1, h, b] = (dq_t * (inverse * SCALE)).T.astype(BF16)
            return inner

        lax.fori_loop(0, 4, one_block, 0)

        def put_back(e, inner):
            back_send[h, e // 4, e % 4] = acc[e // 4, e % 4].astype(BF16)
            return inner

        lax.fori_loop(0, 16, put_back, 0)
        each_sent(lambda n: back_copy(h, n).start())
        hand_out(0, h)
        hand_out(1, h)

        def keep(b, inner):
            own_acc[h, b] = acc[1 + b // 2, 1 + b % 2]
            return inner

        lax.fori_loop(0, 4, keep, 0)
        return carry

    lax.fori_loop(0, GROUP_HEADS, attend, 0)

    def finish(h, carry):
        each_arrival(lambda n: back_copy(h, n).wait_recv())

        def one_block(b, inner):
            bi, bj = b // 2, b % 2
            far_i, far_j = 3 * bi, 3 * bj
            total = own_acc[h, b]
            for i, j in ((far_i, 1 + bj), (1 + bi, far_j), (far_i, far_j)):
                total = total + back_recv[h, i, j].astype(F32)
            low = total.astype(BF16)
            stage[2, h, b] = low[:, :HEAD_DIM]
            stage[3, h, b] = low[:, HEAD_DIM:]
            return inner

        lax.fori_loop(0, 4, one_block, 0)
        hand_out(2, h)
        hand_out(3, h)
        return carry

    lax.fori_loop(0, GROUP_HEADS, finish, 0)

    for a in range(3):
        pair_copy(a).wait_send()
    for n in range(3):
        grad_copy(n).wait_send()

    def sent(h, carry):
        many = pl.ds(0, 16 * (chips - 1))
        pltpu.make_async_copy(recv.at[h, many], recv.at[h, many], all_send_sem.at[h]).wait()
        each_sent(lambda n: halo_copy(h, n).wait_send())
        each_sent(lambda n: back_copy(h, n).wait_send())
        return carry

    lax.fori_loop(0, GROUP_HEADS, sent, 0)
    for o in range(4):
        mine = outs[o].at[:, pl.ds(0, width)]
        far = outs[o].at[:, pl.ds(0, 3 * width)]
        pltpu.make_async_copy(mine, mine, out_sem.at[o]).wait()
        pltpu.make_async_copy(far, far, out_send_sem.at[o]).wait()
        pltpu.make_async_copy(far, far, out_recv_sem.at[o]).wait()


def shards(nt, nh, query_seq, key_seq, value_seq, tile_order, grad_output):
    block_shape = grad_output.shape
    cols = block_shape[2]
    tok, channels = query_seq.shape
    low = jax.ShapeDtypeStruct((tok, channels), BF16)
    hbm = pl.BlockSpec(memory_space=pl.ANY)
    vmem = pl.BlockSpec(memory_space=pltpu.VMEM)
    gh, d = GROUP_HEADS, HEAD_DIM
    dma = pltpu.SemaphoreType.DMA
    outs = pl.pallas_call(
        functools.partial(kernel, nt, nh, cols),
        out_shape=[low] * 4,
        in_specs=[hbm, hbm, hbm, vmem, hbm],
        out_specs=[hbm] * 4,
        scratch_shapes=[
            pltpu.VMEM((3, 2 * tok, 2 * gh * d), BF16),
            pltpu.VMEM((2 * tok, 2 * tok), BF16),
            pltpu.VMEM((gh, 2, 2 * tok, 3 * d), BF16),
            pltpu.VMEM((gh, 4 * tok, 3 * d), BF16),
            pltpu.VMEM((4, tok, 4 * tok), BF16),
            pltpu.VMEM((gh, 4, 4, tok, 2 * d), BF16),
            pltpu.VMEM((4, 4, 2 * d, tok), BF16),
            pltpu.VMEM((gh, 4, d, tok), BF16),
            pltpu.VMEM((4, tok, gh * d), BF16),
            pltpu.VMEM((gh, 4, d, tok), BF16),
            pltpu.VMEM((9, tok, tok), F32),
            pltpu.VMEM((9, tok, tok), BF16),
            pltpu.VMEM((4, 4, tok, 2 * d), F32),
            pltpu.VMEM((gh, 4, tok, 2 * d), F32),
            pltpu.VMEM((gh, 4, 4, tok, 2 * d), BF16),
            pltpu.VMEM((gh, 4, 4, tok, 2 * d), BF16),
            pltpu.VMEM((4, gh, 4, tok, d), BF16),
            dma((3,)), dma((3,)), dma((3,)),
            dma, dma((3,)), dma((3,)),
            dma((gh,)), dma((gh,)), dma((gh,)),
            dma((gh, 8)), dma((gh, 8)), dma((gh, 8)), dma((gh, 8)),
            dma((4,)), dma((4,)), dma((4,)),
        ],
        compiler_params=pltpu.CompilerParams(
            collective_id=0, has_side_effects=True, vmem_limit_bytes=60 * 2**20
        ),
        cost_estimate=pl.CostEstimate(
            flops=12 * 4 * gh * 9 * tok * tok * d,
            bytes_accessed=16 * tok * channels,
            transcendentals=4 * gh * 9 * tok * tok,
        ),
    )(query_seq, key_seq, value_seq, tile_order.reshape(nt * nh, tok), grad_output.reshape(tok, channels))
    return tuple(o.reshape(block_shape) for o in outs)


def solution(mesh):
    seq = P(("ta", "ha"), None)
    grid = P("ta", "ha", None, None)
    return jax.shard_map(
        functools.partial(shards, mesh.shape["ta"], mesh.shape["ha"]),
        mesh=mesh,
        in_specs=(seq, seq, seq, P(), grid),
        out_specs=(grid,) * 4,
        check_vma=False,
    )
```

time: 1360 us -> 189 us (0.14)
  the two profiles are of different devices: /device:TPU:4 before, /device:TPU:33 now
where the time goes in v1:
time: 189 us; the launch traced here: 185 us
  Pallas kernels  177 us (94%)
  local copies, waits for them, and re-layouts  7.45 us (4%)
    pallas_call x1, Pallas kernels, shards(): pl.pallas_call(functools.partial(kernel, nt, nh, cols), out_shape=[low] *...  177 us
    unnamed x10, local copies, waits for them, and re-layouts  5.85 us

profile of v1, /device:TPU:33, one launch (start us, length us, event | category | flops | bytes accessed | tf_op | source)
XLA Modules:
  0.0 185.4 jit_solution(18303867504050232277)
XLA Ops:
  0.6 1.6 reshape.26.order_ref
  2.2 177.3 %shard_map.84 = (bf16[256,1536]{1,0:T(8,128)(2,1)}, bf16[256,1536]{1,0:T(8,128)(2,1)}, bf16[256,1536]{1,0:T(8,128)(2,1)}, bf16[256,1536]{1,0:T(8,128)(2,1)}) custom-call(bf16[256,1536]{1,0:T(8,128)(2,1)} %q_ref.1, bf16[256,1536]{1,0:T(8,128)(2,1)} %k_ref.1, bf16[256,1536]{1,0:T(8,128)(2,1)} %v_ref.1, s32[128,256]{1,0:T(8,128)} %reshape.26.order_ref, ...), custom_call_target="tpu_custom_call" | custom-call | flops 10871635968 | bytes 6291456 | tf_op jit(solution)/shard_map/pallas_call | solution.py:469
  179.5 0.0 copy-start.2
  179.5 2.1 %copy.13 = bf16[4,8,8,1536]{3,2,1,0:T(8,128)(2,1)} copy(bf16[4,8,8,1536]{3,2,1,0:T(8,128)(2,1)} %bitcast.8) | data formatting | bytes 1572864
  181.7 0.0 copy-done.2
  181.7 0.0 copy-start.1
  181.7 0.9 copy.14
  182.5 0.5 copy-done.1
  183.1 0.0 copy-start
  183.1 0.9 copy.15
  184.0 0.5 copy-done
  184.5 0.9 copy.16
Async XLA Ops:
  179.5 2.1 %copy-start.2 = (bf16[256,1536]{1,0:T(8,128)(2,1)S(1)}, bf16[256,1536]{1,0:T(8,128)(2,1)}, u32[]{:S(2)}) copy-start(bf16[256,1536]{1,0:T(8,128)(2,1)} %get-tuple-element.9) | copy-start | bytes 2359300
  181.7 1.4 copy-start.1
  183.1 1.4 copy-start

commit v2 on v1

--- a/solution.py
+++ b/solution.py
@@ -297,11 +297,15 @@
         for n, (dk, dz) in enumerate(DIRECTIONS):
             pl.when(exists(-dk, -dz))(functools.partial(step, n))
 
-    def settle(h, carry):
+    def gather_in(h, carry):
         all_own(h).wait()
         many = pl.ds(0, 16 * (chips - 1))
         pltpu.make_async_copy(recv.at[h, many], recv.at[h, many], all_recv_sem.at[h]).wait()
-
+        return carry
+
+    lax.fori_loop(0, GROUP_HEADS, gather_in, 0)
+
+    def settle(h, carry):
         def one_block(b, inner):
             grid_rows = dot(place[b], recv[h])
             query_t[h, b] = grid_rows[:, :HEAD_DIM].T.astype(BF16)

time: 189 us -> 162 us (0.86); the launches traced: 185 us -> 162 us
  Pallas kernels: 177 us -> 153 us
    pallas_call x1, Pallas kernels: 177 us -> 153 us  [shards(): pl.pallas_call(functools.partial(kernel, nt, nh, cols), out_shape=[low] *...]
where the time goes in v2:
time: 162 us
  Pallas kernels  153 us (94%)
  local copies, waits for them, and re-layouts  7.45 us (5%)
    pallas_call x1, Pallas kernels, shards(): pl.pallas_call(functools.partial(kernel, nt, nh, cols), out_shape=[low] *...  153 us
    unnamed x10, local copies, waits for them, and re-layouts  5.85 us

profile of v2, /device:TPU:33, one launch (start us, length us, event | category | flops | bytes accessed | tf_op | source)
XLA Modules:
  0.0 161.6 jit_solution(2370922950775890129)
XLA Ops:
  0.6 1.6 reshape.26.order_ref
  2.2 153.5 %shard_map.84 = (bf16[256,1536]{1,0:T(8,128)(2,1)}, bf16[256,1536]{1,0:T(8,128)(2,1)}, bf16[256,1536]{1,0:T(8,128)(2,1)}, bf16[256,1536]{1,0:T(8,128)(2,1)}) custom-call(bf16[256,1536]{1,0:T(8,128)(2,1)} %q_ref.1, bf16[256,1536]{1,0:T(8,128)(2,1)} %k_ref.1, bf16[256,1536]{1,0:T(8,128)(2,1)} %v_ref.1, s32[128,256]{1,0:T(8,128)} %reshape.26.order_ref, ...), custom_call_target="tpu_custom_call" | custom-call | flops 10871635968 | bytes 6291456 | tf_op jit(solution)/shard_map/pallas_call | solution.py:473
  155.7 0.0 copy-start.2
  155.7 2.1 %copy.13 = bf16[4,8,8,1536]{3,2,1,0:T(8,128)(2,1)} copy(bf16[4,8,8,1536]{3,2,1,0:T(8,128)(2,1)} %bitcast.8) | data formatting | bytes 1572864
  157.9 0.0 copy-done.2
  157.9 0.0 copy-start.1
  157.9 0.9 copy.14
  158.8 0.5 copy-done.1
  159.3 0.0 copy-start
  159.3 0.9 copy.15
  160.2 0.5 copy-done
  160.7 0.9 copy.16
Async XLA Ops:
  155.7 2.1 %copy-start.2 = (bf16[256,1536]{1,0:T(8,128)(2,1)S(1)}, bf16[256,1536]{1,0:T(8,128)(2,1)}, u32[]{:S(2)}) copy-start(bf16[256,1536]{1,0:T(8,128)(2,1)} %get-tuple-element.9) | copy-start | bytes 2359300
  157.9 1.4 copy-start.1
  159.3 1.4 copy-start

commit v3 on v2

--- a/solution.py
+++ b/solution.py
@@ -18,7 +18,7 @@
 MESH = pl.DeviceIdType.MESH
 F32 = jnp.float32
 BF16 = jnp.bfloat16
-DIRECTIONS = [(a, b) for a in (-1, 0, 1) for b in (-1, 0, 1) if (a, b) != (0, 0)]
+SEAT = {0: 0, 3: 1, 1: 2, 2: 3}
 
 
 def dot(a, b):
@@ -33,24 +33,22 @@
     return lax.broadcasted_iota(jnp.int32, shape, dim)
 
 
-def own_part(step):
-    return {1: 2, -1: 1, 0: pl.ds(1, 2)}[step]
-
-
-def halo_part(step):
-    return {1: 3, -1: 0, 0: pl.ds(1, 2)}[step]
+def spots_of(b):
+    return [(b // 2 + di, b % 2 + dj) for di in range(3) for dj in range(3)]
 
 
 def kernel(
     nt, nh, cols,
     q_ref, k_ref, v_ref, order_ref, grad_ref,
-    att_ref, dq_ref, dk_ref, dv_ref,
+    out_ref,
     pair, sort_one, send, recv, place, ext, ext_t, query_t, grad_blocks, grad_t,
-    score, prob, acc, own_acc, back_send, back_recv, stage,
+    score, prob, grad_score, query_s, grad_s, keep,
+    back_z, from_z, back_x, from_x, stage,
     pair_sem, pair_send_sem, pair_recv_sem,
     grad_sem, grad_send_sem, grad_recv_sem,
     all_sem, all_send_sem, all_recv_sem,
-    halo_send_sem, halo_recv_sem, back_send_sem, back_recv_sem,
+    side_send_sem, side_recv_sem, corner_send_sem, corner_recv_sem,
+    back_z_send_sem, back_z_recv_sem, back_x_send_sem, back_x_recv_sem,
     out_sem, out_send_sem, out_recv_sem,
 ):
     tok = TILE_FRAMES * TILE_ROWS * cols
@@ -66,32 +64,29 @@
     def mate(where):
         return (2 * kk + where[0], 2 * zz + where[1])
 
-    def exists(dk, dz):
-        okay = []
-        if dk < 0:
-            okay.append(kk > 0)
-        if dk > 0:
-            okay.append(kk < nk - 1)
-        if dz < 0:
-            okay.append(zz > 0)
-        if dz > 0:
-            okay.append(zz < nz - 1)
-        return functools.reduce(jnp.logical_and, okay)
-
-    for there, index in (
-        (kk == 0, (0, slice(None))),
-        (kk == nk - 1, (3, slice(None))),
-        (zz == 0, (slice(None), 0)),
-        (zz == nz - 1, (slice(None), 3)),
-    ):
-
-        @pl.when(there)
-        def _():
+    have_x = (kk > 0, kk < nk - 1)
+    have_z = (zz > 0, zz < nz - 1)
+
+    nothing = jnp.zeros((tok, 2 * HEAD_DIM), BF16)
+    for side in range(2):
+
+        @pl.when(jnp.logical_not(have_x[side]))
+        def _(side=side):
             def clear(h, carry):
                 for n in range(4):
-                    at = tuple(n if isinstance(x, slice) else x for x in index)
-                    ext[(h,) + at] = jnp.zeros((tok, 2 * HEAD_DIM), BF16)
-                    back_recv[(h,) + at] = jnp.zeros((tok, 2 * HEAD_DIM), BF16)
+                    ext[h, 3 * side, n] = nothing
+                for n in range(2):
+                    from_x[h, side, n] = nothing
+                return carry
+
+            lax.fori_loop(0, GROUP_HEADS, clear, 0)
+
+        @pl.when(jnp.logical_not(have_z[side]))
+        def _(side=side):
+            def clear(h, carry):
+                for n in range(4):
+                    ext[h, n, 3 * side] = nothing
+                    from_z[h, side, n] = nothing
                 return carry
 
             lax.fori_loop(0, GROUP_HEADS, clear, 0)
@@ -267,35 +262,58 @@
 
     lax.fori_loop(0, 4, turn_grad, 0)
 
-    def halo_copy(h, n):
-        dk, dz = DIRECTIONS[n]
+    def x_device(side):
+        return (ta + 2 * (2 * side - 1), ha)
+
+    def z_device(side):
+        return (ta, ha + 2 * (2 * side - 1))
+
+    def remote(src, dst, sends, recvs, index, device):
         return pltpu.make_async_remote_copy(
-            src_ref=ext.at[h, own_part(dk), own_part(dz)],
-            dst_ref=ext.at[h, halo_part(-dk), halo_part(-dz)],
-            send_sem=halo_send_sem.at[h, n],
-            recv_sem=halo_recv_sem.at[h, n],
-            device_id=(ta + 2 * dk, ha + 2 * dz),
-            device_id_type=MESH,
-        )
-
-    def back_copy(h, n):
-        dk, dz = DIRECTIONS[n]
-        return pltpu.make_async_remote_copy(
-            src_ref=back_send.at[h, halo_part(dk), halo_part(dz)],
-            dst_ref=back_recv.at[h, halo_part(-dk), halo_part(-dz)],
-            send_sem=back_send_sem.at[h, n],
-            recv_sem=back_recv_sem.at[h, n],
-            device_id=(ta + 2 * dk, ha + 2 * dz),
-            device_id_type=MESH,
-        )
-
-    def each_sent(step):
-        for n, (dk, dz) in enumerate(DIRECTIONS):
-            pl.when(exists(dk, dz))(functools.partial(step, n))
-
-    def each_arrival(step):
-        for n, (dk, dz) in enumerate(DIRECTIONS):
-            pl.when(exists(-dk, -dz))(functools.partial(step, n))
+            src_ref=src, dst_ref=dst, send_sem=sends.at[index], recv_sem=recvs.at[index],
+            device_id=device, device_id_type=MESH,
+        )
+
+    def x_side(h, side):
+        return remote(
+            ext.at[h, 1 + side, pl.ds(1, 2)], ext.at[h, 3 - 3 * side, pl.ds(1, 2)],
+            side_send_sem, side_recv_sem, (h, side), x_device(side),
+        )
+
+    def z_side(h, side):
+        return remote(
+            ext.at[h, pl.ds(1, 2), 1 + side], ext.at[h, pl.ds(1, 2), 3 - 3 * side],
+            side_send_sem, side_recv_sem, (h, 2 + side), z_device(side),
+        )
+
+    def corner(h, column, side):
+        return remote(
+            ext.at[h, 3 * column, 1 + side], ext.at[h, 3 * column, 3 - 3 * side],
+            corner_send_sem, corner_recv_sem, (h, 2 * column + side), z_device(side),
+        )
+
+    def z_back(h, side, kind):
+        return remote(
+            back_z.at[h, side, pl.ds(2 * kind, 2)], from_z.at[h, 1 - side, pl.ds(2 * kind, 2)],
+            back_z_send_sem, back_z_recv_sem, (h, 2 * side + kind), z_device(side),
+        )
+
+    def x_back(h, side):
+        return remote(
+            back_x.at[h, side], from_x.at[h, 1 - side],
+            back_x_send_sem, back_x_recv_sem, (h, side), x_device(side),
+        )
+
+    def along(have, step):
+        for side in range(2):
+            pl.when(have[side])(functools.partial(step, side))
+
+    def corners(have, step):
+        for column in range(2):
+            for side in range(2):
+                pl.when(have_x[column] & have[side])(functools.partial(step, column, side))
+
+    came_x, came_z = have_x[::-1], have_z[::-1]
 
     def gather_in(h, carry):
         all_own(h).wait()
@@ -313,129 +331,172 @@
             return inner
 
         lax.fori_loop(0, 4, one_block, 0)
-        each_sent(lambda n: halo_copy(h, n).start())
+        along(have_x, lambda side: x_side(h, side).start())
+
+        @pl.when(h == 0)
+        def _():
+            along(have_z, lambda side: z_side(h, side).start())
+
         return carry
 
     lax.fori_loop(0, GROUP_HEADS, settle, 0)
 
-    outs = (att_ref, dq_ref, dk_ref, dv_ref)
+    def pass_corners(h):
+        along(came_x, lambda side: x_side(h, side).wait_recv())
+        corners(have_z, lambda column, side: corner(h, column, side).start())
+
+    pass_corners(0)
+    along(have_z, lambda side: z_side(1, side).start())
+    pass_corners(1)
+    along(have_z, lambda side: z_side(2, side).start())
 
     def out_cols(h):
         first = ((2 * core + half) * GROUP_HEADS + h) * HEAD_DIM
         return pl.ds(pl.multiple_of(first, HEAD_DIM), HEAD_DIM)
 
-    def out_copy(o, h, n):
-        return pltpu.make_async_remote_copy(
-            src_ref=stage.at[o, h, 2 * others[n][0] + others[n][1]],
-            dst_ref=outs[o].at[:, out_cols(h)],
-            send_sem=out_send_sem.at[o],
-            recv_sem=out_recv_sem.at[o],
-            device_id=mate(others[n]),
-            device_id_type=MESH,
-        )
-
-    def out_own(o, h):
+    def out_copy(pair_of, h, n):
+        two = pl.ds(2 * pair_of, 2)
+        return remote(
+            stage.at[h, 2 * others[n][0] + others[n][1], two], out_ref.at[two, :, out_cols(h)],
+            out_send_sem, out_recv_sem, pair_of, mate(others[n]),
+        )
+
+    def out_own(pair_of, h):
+        two = pl.ds(2 * pair_of, 2)
         return pltpu.make_async_copy(
-            stage.at[o, h, own_block], outs[o].at[:, out_cols(h)], out_sem.at[o]
-        )
-
-    def hand_out(o, h):
-        for n in range(3):
-            out_copy(o, h, n).start()
-        out_own(o, h).start()
+            stage.at[h, own_block, two], out_ref.at[two, :, out_cols(h)], out_sem.at[pair_of]
+        )
+
+    def hand_out(pair_of, h):
+        for n in (1, 2, 0):
+            out_copy(pair_of, h, n).start()
+        out_own(pair_of, h).start()
+
+    def bias_of(i, j):
+        gone = [jnp.logical_not(have_x[i // 3])] if i in (0, 3) else []
+        gone += [jnp.logical_not(have_z[j // 3])] if j in (0, 3) else []
+        if not gone:
+            return None
+        return jnp.where(functools.reduce(jnp.logical_or, gone), NEG, 0.0).astype(F32)
+
+    bias = {(i, j): bias_of(i, j) for i in range(4) for j in range(4)}
 
     def attend(h, carry):
-        each_arrival(lambda n: halo_copy(h, n).wait_recv())
+        along(came_z, lambda side: z_side(h, side).wait_recv())
+        corners(came_z, lambda column, side: corner(h, column, side).wait_recv())
 
         def prepare(e, inner):
             ext_t[e // 4, e % 4] = ext[h, e // 4, e % 4].astype(F32).T.astype(BF16)
-            acc[e // 4, e % 4] = jnp.zeros((tok, 2 * HEAD_DIM), F32)
             return inner
 
         lax.fori_loop(0, 16, prepare, 0)
-
-        def one_block(b, inner):
-            bi, bj = b // 2, b % 2
-            q_t, g_t = query_t[h, b], grad_t[h, b]
-            spots = [(bi + di, bj + dj) for di in range(3) for dj in range(3)]
-            biases = []
-            for i, j in spots:
-                missing = (
-                    ((kk == 0) & (i == 0))
-                    | ((kk == nk - 1) & (i == 3))
-                    | ((zz == 0) & (j == 0))
-                    | ((zz == nz - 1) & (j == 3))
-                )
-                biases.append(jnp.where(missing, NEG, 0.0).astype(F32))
-            top = jnp.full((1, tok), NEG, F32)
-            for n, (i, j) in enumerate(spots):
-                s = dot(ext[h, i, j, :, :HEAD_DIM], q_t)
-                score[n] = s
-                top = jnp.maximum(top, jnp.max(s, axis=0, keepdims=True) + biases[n])
-            shift = top * (SCALE * LOG2E)
-            total = jnp.zeros((1, tok), F32)
-            out_t = jnp.zeros((HEAD_DIM, tok), F32)
-            for n, (i, j) in enumerate(spots):
-                p = jnp.exp2(score[n] * (SCALE * LOG2E) - (shift - biases[n]))
-                total = total + jnp.sum(p, axis=0, keepdims=True)
-                p_low = p.astype(BF16)
-                prob[n] = p_low
-                out_t = out_t + dot(ext_t[i, j, HEAD_DIM:, :], p_low)
-            inverse = 1.0 / total
-            out_t = out_t * inverse
-            grad_f = g_t.astype(F32)
-            delta = jnp.sum(grad_f * out_t, axis=0, keepdims=True)
-            stage[0, h, b] = out_t.T.astype(BF16)
-            g_scaled = (grad_f * inverse).astype(BF16)
-            q_scaled = (q_t.astype(F32) * (inverse * SCALE)).astype(BF16)
-            dq_t = jnp.zeros((HEAD_DIM, tok), F32)
-            for n, (i, j) in enumerate(spots):
-                dp = dot(ext[h, i, j, :, HEAD_DIM:], g_t)
-                p_low = prob[n]
-                ds = (p_low.astype(F32) * (dp - delta)).astype(BF16)
-                dq_t = dq_t + dot(ext_t[i, j, :HEAD_DIM, :], ds)
-                acc[i, j, :, :HEAD_DIM] += dot_nt(ds, q_scaled)
-                acc[i, j, :, HEAD_DIM:] += dot_nt(p_low, g_scaled)
-            stage[1, h, b] = (dq_t * (inverse * SCALE)).T.astype(BF16)
-            return inner
-
-        lax.fori_loop(0, 4, one_block, 0)
-
-        def put_back(e, inner):
-            back_send[h, e // 4, e % 4] = acc[e // 4, e % 4].astype(BF16)
-            return inner
-
-        lax.fori_loop(0, 16, put_back, 0)
-        each_sent(lambda n: back_copy(h, n).start())
+        top, total, out_t, dq_t = [None] * 4, [None] * 4, [None] * 4, [None] * 4
+        delta, inverse = [None] * 4, [None] * 4
+
+        def add(held, b, n, term):
+            held[b] = term if n == 0 else held[b] + term
+
+        def scores_of(b, n):
+            spot = spots_of(b)[n]
+            s = dot(ext[h, spot[0], spot[1], :, :HEAD_DIM], query_t[h, b])
+            score[b % 2, n] = s
+            most = jnp.max(s, axis=0, keepdims=True)
+            if bias[spot] is not None:
+                most = most + bias[spot]
+            top[b] = most if n == 0 else jnp.maximum(top[b], most)
+
+        def forward(b, n):
+            i, j = spots_of(b)[n]
+            shift = top[b] * (SCALE * LOG2E)
+            if bias[i, j] is not None:
+                shift = shift - bias[i, j]
+            p = jnp.exp2(score[b % 2, n] * (SCALE * LOG2E) - shift)
+            add(total, b, n, jnp.sum(p, axis=0, keepdims=True))
+            p_low = p.astype(BF16)
+            prob[b, n] = p_low
+            add(out_t, b, n, dot(ext_t[i, j, HEAD_DIM:, :], p_low))
+            if n == 8:
+                inverse[b] = 1.0 / total[b]
+                full = out_t[b] * inverse[b]
+                grad_f = grad_t[h, b].astype(F32)
+                delta[b] = jnp.sum(grad_f * full, axis=0, keepdims=True)
+                stage[h, b, 0] = full.T.astype(BF16)
+                grad_s[b] = (grad_f * inverse[b]).astype(BF16)
+                query_s[b] = (query_t[h, b].astype(F32) * (inverse[b] * SCALE)).astype(BF16)
+
+        def backward(b, n):
+            i, j = spots_of(b)[n]
+            dp = dot(ext[h, i, j, :, HEAD_DIM:], grad_t[h, b])
+            ds = (prob[b, n].astype(F32) * (dp - delta[b])).astype(BF16)
+            grad_score[b, n] = ds
+            add(dq_t, b, n, dot(ext_t[i, j, :HEAD_DIM, :], ds))
+            if n == 8:
+                stage[h, b, 1] = (dq_t[b] * (inverse[b] * SCALE)).T.astype(BF16)
+
+        for turn in range(6):
+            for n in range(9):
+                for step, b in ((scores_of, turn), (forward, turn - 1), (backward, turn - 2)):
+                    if 0 <= b < 4:
+                        step(b, n)
+
+        def key_terms(i, j):
+            k_sum = v_sum = None
+            for b in range(4):
+                if (i, j) in spots_of(b):
+                    n = spots_of(b).index((i, j))
+                    k_term = dot_nt(grad_score[b, n], query_s[b])
+                    v_term = dot_nt(prob[b, n], grad_s[b])
+                    k_sum = k_term if k_sum is None else k_sum + k_term
+                    v_sum = v_term if v_sum is None else v_sum + v_term
+            return ((slice(0, HEAD_DIM), k_sum), (slice(HEAD_DIM, 2 * HEAD_DIM), v_sum))
+
+        for kind in range(2):
+            for side in range(2):
+                for i in ((0, 3), (1, 2))[kind]:
+                    for lanes, value in key_terms(i, 3 * side):
+                        back_z[h, side, SEAT[i], :, lanes] = value.astype(BF16)
+            along(have_z, lambda side: z_back(h, side, kind).start())
         hand_out(0, h)
+        for i in (0, 3, 1, 2):
+            for j in (1, 2):
+                for lanes, value in key_terms(i, j):
+                    keep[h, i, j - 1, :, lanes] = value
+        return carry
+
+    def turn_x(h):
+        along(came_z, lambda side: z_back(h, side, 0).wait_recv())
+        for side in range(2):
+            for j in range(2):
+                both = keep[h, 3 * side, j] + from_z[h, j, side].astype(F32)
+                back_x[h, side, j] = both.astype(BF16)
+        along(have_x, lambda side: x_back(h, side).start())
+
+    def heads(h, carry):
+        attend(h, 0)
+
+        @pl.when(h == 0)
+        def _():
+            pass_corners(GROUP_HEADS - 1)
+
+        @pl.when(h > 0)
+        def _():
+            turn_x(h - 1)
+
+        return carry
+
+    lax.fori_loop(0, GROUP_HEADS, heads, 0)
+    turn_x(GROUP_HEADS - 1)
+
+    def finish(h, carry):
+        along(came_z, lambda side: z_back(h, side, 1).wait_recv())
+        along(came_x, lambda side: x_back(h, side).wait_recv())
+        for b in range(4):
+            i, j = b // 2, b % 2
+            whole = keep[h, 1 + i, j] + from_z[h, j, 2 + i].astype(F32)
+            low = (whole + from_x[h, i, j].astype(F32)).astype(BF16)
+            stage[h, b, 2] = low[:, :HEAD_DIM]
+            stage[h, b, 3] = low[:, HEAD_DIM:]
         hand_out(1, h)
-
-        def keep(b, inner):
-            own_acc[h, b] = acc[1 + b // 2, 1 + b % 2]
-            return inner
-
-        lax.fori_loop(0, 4, keep, 0)
-        return carry
-
-    lax.fori_loop(0, GROUP_HEADS, attend, 0)
-
-    def finish(h, carry):
-        each_arrival(lambda n: back_copy(h, n).wait_recv())
-
-        def one_block(b, inner):
-            bi, bj = b // 2, b % 2
-            far_i, far_j = 3 * bi, 3 * bj
-            total = own_acc[h, b]
-            for i, j in ((far_i, 1 + bj), (1 + bi, far_j), (far_i, far_j)):
-                total = total + back_recv[h, i, j].astype(F32)
-            low = total.astype(BF16)
-            stage[2, h, b] = low[:, :HEAD_DIM]
-            stage[3, h, b] = low[:, HEAD_DIM:]
-            return inner
-
-        lax.fori_loop(0, 4, one_block, 0)
-        hand_out(2, h)
-        hand_out(3, h)
         return carry
 
     lax.fori_loop(0, GROUP_HEADS, finish, 0)
@@ -448,17 +509,31 @@
     def sent(h, carry):
         many = pl.ds(0, 16 * (chips - 1))
         pltpu.make_async_copy(recv.at[h, many], recv.at[h, many], all_send_sem.at[h]).wait()
-        each_sent(lambda n: halo_copy(h, n).wait_send())
-        each_sent(lambda n: back_copy(h, n).wait_send())
+        along(have_x, lambda side: x_side(h, side).wait_send())
+        along(have_z, lambda side: z_side(h, side).wait_send())
+        corners(have_z, lambda column, side: corner(h, column, side).wait_send())
+        for kind in range(2):
+            along(have_z, lambda side: z_back(h, side, kind).wait_send())
+        along(have_x, lambda side: x_back(h, side).wait_send())
         return carry
 
     lax.fori_loop(0, GROUP_HEADS, sent, 0)
-    for o in range(4):
-        mine = outs[o].at[:, pl.ds(0, width)]
-        far = outs[o].at[:, pl.ds(0, 3 * width)]
-        pltpu.make_async_copy(mine, mine, out_sem.at[o]).wait()
-        pltpu.make_async_copy(far, far, out_send_sem.at[o]).wait()
-        pltpu.make_async_copy(far, far, out_recv_sem.at[o]).wait()
+    for pair_of in range(2):
+        two = pl.ds(2 * pair_of, 2)
+        mine = out_ref.at[two, :, pl.ds(0, width)]
+        far = out_ref.at[two, :, pl.ds(0, 3 * width)]
+        pltpu.make_async_copy(mine, mine, out_sem.at[pair_of]).wait()
+        pltpu.make_async_copy(far, far, out_send_sem.at[pair_of]).wait()
+        pltpu.make_async_copy(far, far, out_recv_sem.at[pair_of]).wait()
+
+
+def deal(in_ref, *refs):
+    outs, sems = refs[:4], refs[4]
+    copies = [pltpu.make_async_copy(in_ref.at[n], outs[n], sems.at[n]) for n in range(4)]
+    for copy in copies:
+        copy.start()
+    for copy in copies:
+        copy.wait()
 
 
 def shards(nt, nh, query_seq, key_seq, value_seq, tile_order, grad_output):
@@ -470,11 +545,11 @@
     vmem = pl.BlockSpec(memory_space=pltpu.VMEM)
     gh, d = GROUP_HEADS, HEAD_DIM
     dma = pltpu.SemaphoreType.DMA
-    outs = pl.pallas_call(
+    whole = pl.pallas_call(
         functools.partial(kernel, nt, nh, cols),
-        out_shape=[low] * 4,
+        out_shape=jax.ShapeDtypeStruct((4, tok, channels), BF16),
         in_specs=[hbm, hbm, hbm, vmem, hbm],
-        out_specs=[hbm] * 4,
+        out_specs=hbm,
         scratch_shapes=[
             pltpu.VMEM((3, 2 * tok, 2 * gh * d), BF16),
             pltpu.VMEM((2 * tok, 2 * tok), BF16),
@@ -486,18 +561,23 @@
             pltpu.VMEM((gh, 4, d, tok), BF16),
             pltpu.VMEM((4, tok, gh * d), BF16),
             pltpu.VMEM((gh, 4, d, tok), BF16),
-            pltpu.VMEM((9, tok, tok), F32),
-            pltpu.VMEM((9, tok, tok), BF16),
-            pltpu.VMEM((4, 4, tok, 2 * d), F32),
-            pltpu.VMEM((gh, 4, tok, 2 * d), F32),
-            pltpu.VMEM((gh, 4, 4, tok, 2 * d), BF16),
-            pltpu.VMEM((gh, 4, 4, tok, 2 * d), BF16),
-            pltpu.VMEM((4, gh, 4, tok, d), BF16),
+            pltpu.VMEM((2, 9, tok, tok), F32),
+            pltpu.VMEM((4, 9, tok, tok), BF16),
+            pltpu.VMEM((4, 9, tok, tok), BF16),
+            pltpu.VMEM((4, d, tok), BF16),
+            pltpu.VMEM((4, d, tok), BF16),
+            pltpu.VMEM((gh, 4, 2, tok, 2 * d), F32),
+            pltpu.VMEM((gh, 2, 4, tok, 2 * d), BF16),
+            pltpu.VMEM((gh, 2, 4, tok, 2 * d), BF16),
+            pltpu.VMEM((gh, 2, 2, tok, 2 * d), BF16),
+            pltpu.VMEM((gh, 2, 2, tok, 2 * d), BF16),
+            pltpu.VMEM((gh, 4, 4, tok, d), BF16),
             dma((3,)), dma((3,)), dma((3,)),
             dma, dma((3,)), dma((3,)),
             dma((gh,)), dma((gh,)), dma((gh,)),
-            dma((gh, 8)), dma((gh, 8)), dma((gh, 8)), dma((gh, 8)),
-            dma((4,)), dma((4,)), dma((4,)),
+            dma((gh, 4)), dma((gh, 4)), dma((gh, 4)), dma((gh, 4)),
+            dma((gh, 4)), dma((gh, 4)), dma((gh, 2)), dma((gh, 2)),
+            dma((2,)), dma((2,)), dma((2,)),
         ],
         compiler_params=pltpu.CompilerParams(
             collective_id=0, has_side_effects=True, vmem_limit_bytes=60 * 2**20
@@ -508,6 +588,13 @@
             transcendentals=4 * gh * 9 * tok * tok,
         ),
     )(query_seq, key_seq, value_seq, tile_order.reshape(nt * nh, tok), grad_output.reshape(tok, channels))
+    outs = pl.pallas_call(
+        deal,
+        out_shape=[low] * 4,
+        in_specs=[hbm],
+        out_specs=[hbm] * 4,
+        scratch_shapes=[dma((4,))],
+    )(whole)
     return tuple(o.reshape(block_shape) for o in outs)
 
 

time: 162 us -> 235 us (1.45)
  Pallas kernels: 153 us -> 232 us
  local copies, waits for them, and re-layouts: 7.45 us -> 1.6 us
    pallas_call x1 -> x2, Pallas kernels: 153 us -> 232 us  [the longest x1 136 us: shards(): pl.pallas_call(functools.partial(kernel, nt, nh, cols), out_shape=jax.Sha...]
    unnamed x10 -> x0, local copies, waits for them, and re-layouts: 5.85 us -> none
where the time goes in v3:
time: 235 us
  Pallas kernels  232 us (99%)
    pallas_call x1, Pallas kernels, shards(): pl.pallas_call(functools.partial(kernel, nt, nh, cols), out_shape=jax.Sha...  136 us
    pallas_call x1, Pallas kernels, shards(): pl.pallas_call(deal, out_shape=[low] * 4, in_specs=[hbm], out_specs=[hbm]...  96.4 us

profile of v3, /device:TPU:33, one launch (start us, length us, event | category | flops | bytes accessed | tf_op | source)
XLA Modules:
  0.0 234.7 jit_solution(16535109569527688791)
XLA Ops:
  0.6 1.6 reshape.26.order_ref
  2.2 135.9 %shard_map.84.in_ref = bf16[4,256,1536]{2,1,0:T(8,128)(2,1)} custom-call(bf16[256,1536]{1,0:T(8,128)(2,1)} %q_ref.1, bf16[256,1536]{1,0:T(8,128)(2,1)} %k_ref.1, bf16[256,1536]{1,0:T(8,128)(2,1)} %v_ref.1, s32[128,256]{1,0:T(8,128)} %reshape.26.order_ref, bf16[256,1536]{1,0:T(8,128)(2,1)} %bitcast.5), custom_call_target="tpu_custom_call" | custom-call | flops 10871635968 | bytes 6291456 | tf_op jit(solution)/shard_map/pallas_call | solution.py:548
  138.1 96.4 %shard_map.85 = (bf16[256,1536]{1,0:T(8,128)(2,1)}, bf16[256,1536]{1,0:T(8,128)(2,1)}, bf16[256,1536]{1,0:T(8,128)(2,1)}, bf16[256,1536]{1,0:T(8,128)(2,1)}) custom-call(bf16[4,256,1536]{2,1,0:T(8,128)(2,1)} %shard_map.84.in_ref), custom_call_target="tpu_custom_call" | custom-call | tf_op jit(solution)/shard_map/pallas_call | solution.py:591

commit v4 on v3

--- a/solution.py
+++ b/solution.py
@@ -528,11 +528,15 @@
 
 
 def deal(in_ref, *refs):
-    outs, sems = refs[:4], refs[4]
-    copies = [pltpu.make_async_copy(in_ref.at[n], outs[n], sems.at[n]) for n in range(4)]
-    for copy in copies:
+    outs, (held, in_sem, out_sem) = refs[:4], refs[4:]
+    into = [pltpu.make_async_copy(in_ref.at[n], held.at[n], in_sem.at[n]) for n in range(4)]
+    onward = [pltpu.make_async_copy(held.at[n], outs[n], out_sem.at[n]) for n in range(4)]
+    for copy in into:
         copy.start()
-    for copy in copies:
+    for n in range(4):
+        into[n].wait()
+        onward[n].start()
+    for copy in onward:
         copy.wait()
 
 
@@ -593,7 +597,8 @@
         out_shape=[low] * 4,
         in_specs=[hbm],
         out_specs=[hbm] * 4,
-        scratch_shapes=[dma((4,))],
+        scratch_shapes=[pltpu.VMEM((4, tok, channels), BF16), dma((4,)), dma((4,))],
+        compiler_params=pltpu.CompilerParams(vmem_limit_bytes=60 * 2**20),
     )(whole)
     return tuple(o.reshape(block_shape) for o in outs)
 

time: 235 us -> 141 us (0.60)
  Pallas kernels: 232 us -> 139 us
    pallas_call x1, Pallas kernels: 96.4 us -> 2.86 us  [shards(): pl.pallas_call(deal, out_shape=[low] * 4, in_specs=[hbm], out_specs=[hbm]...]
where the time goes in v4:
time: 141 us
  Pallas kernels  139 us (99%)
  local copies, waits for them, and re-layouts  1.6 us (1%)
    pallas_call x1, Pallas kernels, shards(): pl.pallas_call(functools.partial(kernel, nt, nh, cols), out_shape=jax.Sha...  136 us
    pallas_call x1, Pallas kernels, shards(): pl.pallas_call(deal, out_shape=[low] * 4, in_specs=[hbm], out_specs=[hbm]...  2.86 us

profile of v4, /device:TPU:33, one launch (start us, length us, event | category | flops | bytes accessed | tf_op | source)
XLA Modules:
  0.0 141.2 jit_solution(15710847939660330845)
XLA Ops:
  0.6 1.6 %reshape.26.order_ref = s32[128,256]{1,0:T(8,128)} reshape(s32[32768]{0:T(1024)} %param.8) | data formatting | bytes 262144 | tf_op jit(solution)/shard_map/reshape | solution.py:594
  2.2 135.9 %shard_map.84.in_ref = bf16[4,256,1536]{2,1,0:T(8,128)(2,1)} custom-call(bf16[256,1536]{1,0:T(8,128)(2,1)} %q_ref.1, bf16[256,1536]{1,0:T(8,128)(2,1)} %k_ref.1, bf16[256,1536]{1,0:T(8,128)(2,1)} %v_ref.1, s32[128,256]{1,0:T(8,128)} %reshape.26.order_ref, bf16[256,1536]{1,0:T(8,128)(2,1)} %bitcast.5), custom_call_target="tpu_custom_call" | custom-call | flops 10871635968 | bytes 6291456 | tf_op jit(solution)/shard_map/pallas_call | solution.py:552
  138.1 2.9 %shard_map.85 = (bf16[256,1536]{1,0:T(8,128)(2,1)}, bf16[256,1536]{1,0:T(8,128)(2,1)}, bf16[256,1536]{1,0:T(8,128)(2,1)}, bf16[256,1536]{1,0:T(8,128)(2,1)}) custom-call(bf16[4,256,1536]{2,1,0:T(8,128)(2,1)} %shard_map.84.in_ref), custom_call_target="tpu_custom_call" | custom-call | tf_op jit(solution)/shard_map/pallas_call | solution.py:595

commit v5 on v4

--- a/solution.py
+++ b/solution.py
@@ -42,13 +42,14 @@
     q_ref, k_ref, v_ref, order_ref, grad_ref,
     out_ref,
     pair, sort_one, send, recv, place, ext, ext_t, query_t, grad_blocks, grad_t,
-    score, prob, grad_score, query_s, grad_s, keep,
-    back_z, from_z, back_x, from_x, stage,
+    score, prob, grad_score, query_s, grad_s, keep, keep_z,
+    back_z, from_z, back_x, from_x, back_cross, from_cross, stage,
     pair_sem, pair_send_sem, pair_recv_sem,
     grad_sem, grad_send_sem, grad_recv_sem,
     all_sem, all_send_sem, all_recv_sem,
-    side_send_sem, side_recv_sem, corner_send_sem, corner_recv_sem,
+    side_send_sem, side_recv_sem, corner_send_sem, corner_recv_sem, cross_send_sem,
     back_z_send_sem, back_z_recv_sem, back_x_send_sem, back_x_recv_sem,
+    back_cross_send_sem, back_cross_recv_sem,
     out_sem, out_send_sem, out_recv_sem,
 ):
     tok = TILE_FRAMES * TILE_ROWS * cols
@@ -66,6 +67,9 @@
 
     have_x = (kk > 0, kk < nk - 1)
     have_z = (zz > 0, zz < nz - 1)
+    far_x = (kk == nk // 2, kk == nk // 2 - 1)
+    half_tok = tok // 2
+    part_rows = (pl.ds(0, half_tok), pl.ds(half_tok, half_tok))
 
     nothing = jnp.zeros((tok, 2 * HEAD_DIM), BF16)
     for side in range(2):
@@ -81,6 +85,15 @@
 
             lax.fori_loop(0, GROUP_HEADS, clear, 0)
 
+        @pl.when(jnp.logical_not(have_x[side]) | far_x[side])
+        def _(side=side):
+            def clear(h, carry):
+                for n in range(2):
+                    from_cross[h, side, n] = jnp.zeros((half_tok, 2 * HEAD_DIM), BF16)
+                return carry
+
+            lax.fori_loop(0, GROUP_HEADS, clear, 0)
+
         @pl.when(jnp.logical_not(have_z[side]))
         def _(side=side):
             def clear(h, carry):
@@ -105,14 +118,25 @@
         pl.semaphore_signal(barrier, inc=1, device_id=mate(where), device_id_type=MESH)
 
     seq = (q_ref, k_ref, v_ref)
-    pair_width = 2 * width
-    own_cols = pl.ds(pl.multiple_of(core * pair_width, pair_width), pair_width)
-    far_cols = pl.ds(pl.multiple_of((1 - core) * pair_width, pair_width), pair_width)
     own_rows = pl.ds(pl.multiple_of(core * tok, tok), tok)
-    for a in range(3):
-        pltpu.make_async_copy(
-            seq[a].at[:, own_cols], pair.at[a, own_rows], pair_sem.at[a]
-        ).start()
+
+    def head_cols(h, n, of):
+        inner = (n % 2) * width + h * HEAD_DIM
+        return pl.ds(pl.multiple_of(of * 2 * width + inner, HEAD_DIM), HEAD_DIM)
+
+    def pair_own(h, n):
+        return pltpu.make_async_copy(
+            seq[n // 2].at[:, head_cols(h, n, core)],
+            pair.at[n // 2, own_rows, head_cols(h, n, 0)],
+            pair_sem.at[h, n],
+        )
+
+    def start_own(h, carry):
+        for n in range(6):
+            pair_own(h, n).start()
+        return carry
+
+    lax.fori_loop(0, GROUP_HEADS, start_own, 0)
 
     def group_cols(where, n=width):
         return pl.ds(pl.multiple_of((2 * where[0] + where[1]) * width, width), width)
@@ -124,12 +148,12 @@
 
     pl.semaphore_wait(barrier, chips + 1)
 
-    def pair_copy(a):
+    def pair_copy(h, n):
         return pltpu.make_async_remote_copy(
-            src_ref=seq[a].at[:, far_cols],
-            dst_ref=pair.at[a, own_rows],
-            send_sem=pair_send_sem.at[a],
-            recv_sem=pair_recv_sem.at[a],
+            src_ref=seq[n // 2].at[:, head_cols(h, n, 1 - core)],
+            dst_ref=pair.at[n // 2, own_rows, head_cols(h, n, 0)],
+            send_sem=pair_send_sem.at[h, n],
+            recv_sem=pair_recv_sem.at[h, n],
             device_id=mate((1 - core, half)),
             device_id_type=MESH,
         )
@@ -144,8 +168,12 @@
             device_id_type=MESH,
         )
 
-    for a in range(3):
-        pair_copy(a).start()
+    def start_pair(h, carry):
+        for n in range(6):
+            pair_copy(h, n).start()
+        return carry
+
+    lax.fori_loop(0, GROUP_HEADS, start_pair, 0)
     for n in range(3):
         grad_copy(n).start()
 
@@ -174,12 +202,6 @@
         sort_one[:, cc * tok : (cc + 1) * tok] = jnp.where(
             iota((2 * tok, tok), 0) == seat, 1.0, 0.0
         ).astype(BF16)
-
-    for a in range(3):
-        pltpu.make_async_copy(
-            seq[a].at[:, own_cols], pair.at[a, own_rows], pair_sem.at[a]
-        ).wait()
-        pair_copy(a).wait_recv()
 
     def all_copy(h, d):
         to = lax.rem(chip + d, chips)
@@ -203,6 +225,9 @@
         )
 
     def send_head(h, carry):
+        for n in range(6):
+            pair_own(h, n).wait()
+            pair_copy(h, n).wait_recv()
         for a in range(3):
             left = pl.ds(pl.multiple_of(h * HEAD_DIM, HEAD_DIM), HEAD_DIM)
             right = pl.ds(pl.multiple_of(width + h * HEAD_DIM, HEAD_DIM), HEAD_DIM)
@@ -286,34 +311,65 @@
             side_send_sem, side_recv_sem, (h, 2 + side), z_device(side),
         )
 
-    def corner(h, column, side):
+    def corner(h, column, side, part):
         return remote(
-            ext.at[h, 3 * column, 1 + side], ext.at[h, 3 * column, 3 - 3 * side],
-            corner_send_sem, corner_recv_sem, (h, 2 * column + side), z_device(side),
-        )
-
-    def z_back(h, side, kind):
+            ext.at[h, 3 * column, 1 + side, part_rows[part]],
+            ext.at[h, 3 * column, 3 - 3 * side, part_rows[part]],
+            corner_send_sem, corner_recv_sem, (h, 4 * part + 2 * column + side), z_device(side),
+        )
+
+    def cross(h, column, side):
+        return pltpu.make_async_remote_copy(
+            src_ref=ext.at[h, 1 + column, 3 * side, part_rows[1]],
+            dst_ref=ext.at[h, 3 - 3 * column, 3 * side, part_rows[1]],
+            send_sem=cross_send_sem.at[h, 2 * column + side],
+            recv_sem=corner_recv_sem.at[h, 4 + 2 * (1 - column) + 1 - side],
+            device_id=x_device(column),
+            device_id_type=MESH,
+        )
+
+    def z_back(h, side, kind, part):
+        two = pl.ds(2 * kind, 2)
         return remote(
-            back_z.at[h, side, pl.ds(2 * kind, 2)], from_z.at[h, 1 - side, pl.ds(2 * kind, 2)],
-            back_z_send_sem, back_z_recv_sem, (h, 2 * side + kind), z_device(side),
-        )
-
-    def x_back(h, side):
+            back_z.at[h, side, two, part_rows[part]], from_z.at[h, 1 - side, two, part_rows[part]],
+            back_z_send_sem, back_z_recv_sem, (h, 2 * (kind + part) + side), z_device(side),
+        )
+
+    def z_back_far(h, column, side):
         return remote(
-            back_x.at[h, side], from_x.at[h, 1 - side],
-            back_x_send_sem, back_x_recv_sem, (h, side), x_device(side),
+            back_z.at[h, side, column, part_rows[1]], from_z.at[h, 1 - side, column, part_rows[1]],
+            back_z_send_sem, back_z_recv_sem, (h, 6 + 2 * column + side), z_device(side),
+        )
+
+    def x_back(h, side, part):
+        both = pl.ds(0, 2)
+        return remote(
+            back_x.at[h, side, both, part_rows[part]], from_x.at[h, 1 - side, both, part_rows[part]],
+            back_x_send_sem, back_x_recv_sem, (h, 2 * part + side), x_device(side),
+        )
+
+    def x_cross(h, column, side):
+        return remote(
+            back_cross.at[h, column, side], from_cross.at[h, 1 - column, side],
+            back_cross_send_sem, back_cross_recv_sem, (h, 2 * column + side), x_device(column),
         )
 
     def along(have, step):
         for side in range(2):
             pl.when(have[side])(functools.partial(step, side))
 
-    def corners(have, step):
+    def corners(have, step, only=None):
         for column in range(2):
             for side in range(2):
-                pl.when(have_x[column] & have[side])(functools.partial(step, column, side))
-
+                when = have_x[column] & have[side]
+                if only is not None:
+                    when = when & only[column]
+                pl.when(when)(functools.partial(step, column, side))
+
+    near_x = tuple(jnp.logical_not(f) for f in far_x)
     came_x, came_z = have_x[::-1], have_z[::-1]
+    at_near = tuple(have_x[n] & near_x[n] for n in range(2))
+    at_far = tuple(have_x[n] & far_x[n] for n in range(2))
 
     def gather_in(h, carry):
         all_own(h).wait()
@@ -322,6 +378,10 @@
         return carry
 
     lax.fori_loop(0, GROUP_HEADS, gather_in, 0)
+
+    def start_sides(h):
+        along(have_x, lambda side: x_side(h, side).start())
+        along(have_z, lambda side: z_side(h, side).start())
 
     def settle(h, carry):
         def one_block(b, inner):
@@ -331,24 +391,21 @@
             return inner
 
         lax.fori_loop(0, 4, one_block, 0)
-        along(have_x, lambda side: x_side(h, side).start())
-
-        @pl.when(h == 0)
-        def _():
-            along(have_z, lambda side: z_side(h, side).start())
-
+        pl.when(h == 0)(lambda: start_sides(0))
         return carry
 
     lax.fori_loop(0, GROUP_HEADS, settle, 0)
 
     def pass_corners(h):
         along(came_x, lambda side: x_side(h, side).wait_recv())
-        corners(have_z, lambda column, side: corner(h, column, side).start())
+        corners(have_z, lambda column, side: corner(h, column, side, 0).start())
+        corners(have_z, lambda column, side: corner(h, column, side, 1).start(), far_x)
+        along(came_z, lambda side: z_side(h, side).wait_recv())
+        corners(have_z, lambda column, side: cross(h, column, side).start(), near_x)
 
     pass_corners(0)
-    along(have_z, lambda side: z_side(1, side).start())
-    pass_corners(1)
-    along(have_z, lambda side: z_side(2, side).start())
+    start_sides(1)
+    start_sides(2)
 
     def out_cols(h):
         first = ((2 * core + half) * GROUP_HEADS + h) * HEAD_DIM
@@ -381,9 +438,49 @@
 
     bias = {(i, j): bias_of(i, j) for i in range(4) for j in range(4)}
 
+    def turn(h):
+        first, later = slice(0, half_tok), slice(half_tok, tok)
+        along(came_z, lambda side: z_back(h, side, 0, 0).wait_recv())
+        for column in range(2):
+            for j in range(2):
+                both = keep[h, 3 * column, j, first] + from_z[h, j, column, first].astype(F32)
+                back_x[h, column, j, first] = both.astype(BF16)
+        along(have_x, lambda side: x_back(h, side, 0).start())
+        corners(came_z, lambda column, side: z_back_far(h, column, side).wait_recv(), far_x)
+
+        def add_far(column):
+            for j in range(2):
+                both = keep[h, 3 * column, j, later] + from_z[h, j, column, later].astype(F32)
+                back_x[h, column, j, later] = both.astype(BF16)
+            x_back(h, column, 1).start()
+
+        along(at_far, add_far)
+        for column in range(2):
+            for side in range(2):
+                pl.when(at_near[1 - column] & have_z[side])(
+                    functools.partial(lambda c, d: x_cross(h, c, d).wait_recv(), column, side)
+                )
+        for side in range(2):
+            for i in range(2):
+                both = keep_z[h, side, i] + from_cross[h, i, side].astype(F32)
+                back_z[h, side, 2 + i, later] = both.astype(BF16)
+        along(have_z, lambda side: z_back(h, side, 1, 1).start())
+
+    def finish(h):
+        for part in range(2):
+            along(came_z, lambda side: z_back(h, side, 1, part).wait_recv())
+            along(came_x, lambda side: x_back(h, side, part).wait_recv())
+        for b in range(4):
+            i, j = b // 2, b % 2
+            whole = keep[h, 1 + i, j] + from_z[h, j, 2 + i].astype(F32)
+            low = (whole + from_x[h, i, j].astype(F32)).astype(BF16)
+            stage[h, b, 2] = low[:, :HEAD_DIM]
+            stage[h, b, 3] = low[:, HEAD_DIM:]
+        hand_out(1, h)
+
     def attend(h, carry):
-        along(came_z, lambda side: z_side(h, side).wait_recv())
-        corners(came_z, lambda column, side: corner(h, column, side).wait_recv())
+        for part in range(2):
+            corners(came_z, lambda column, side: corner(h, column, side, part).wait_recv())
 
         def prepare(e, inner):
             ext_t[e // 4, e % 4] = ext[h, e // 4, e % 4].astype(F32).T.astype(BF16)
@@ -433,11 +530,16 @@
             if n == 8:
                 stage[h, b, 1] = (dq_t[b] * (inverse[b] * SCALE)).T.astype(BF16)
 
-        for turn in range(6):
+        for beat in range(6):
             for n in range(9):
-                for step, b in ((scores_of, turn), (forward, turn - 1), (backward, turn - 2)):
+                for step, b in ((scores_of, beat), (forward, beat - 1), (backward, beat - 2)):
                     if 0 <= b < 4:
                         step(b, n)
+
+        hand_out(0, h)
+
+        pl.when(h == 0)(lambda: pass_corners(1))
+        pl.when(h > 0)(lambda: turn(h - 1))
 
         def key_terms(i, j):
             k_sum = v_sum = None
@@ -450,71 +552,59 @@
                     v_sum = v_term if v_sum is None else v_sum + v_term
             return ((slice(0, HEAD_DIM), k_sum), (slice(HEAD_DIM, 2 * HEAD_DIM), v_sum))
 
-        for kind in range(2):
-            for side in range(2):
-                for i in ((0, 3), (1, 2))[kind]:
-                    for lanes, value in key_terms(i, 3 * side):
-                        back_z[h, side, SEAT[i], :, lanes] = value.astype(BF16)
-            along(have_z, lambda side: z_back(h, side, kind).start())
-        hand_out(0, h)
-        for i in (0, 3, 1, 2):
+        first, later = slice(0, half_tok), slice(half_tok, tok)
+        for side in range(2):
+            for column in range(2):
+                for lanes, value in key_terms(3 * column, 3 * side):
+                    low = value.astype(BF16)
+                    back_z[h, side, column, :, lanes] = low
+                    back_cross[h, column, side, :, lanes] = low[later]
+        along(have_z, lambda side: z_back(h, side, 0, 0).start())
+        corners(have_z, lambda column, side: z_back_far(h, column, side).start(), far_x)
+        corners(have_z, lambda column, side: x_cross(h, column, side).start(), near_x)
+        for column in range(2):
+            for j in (1, 2):
+                for lanes, value in key_terms(3 * column, j):
+                    keep[h, 3 * column, j - 1, :, lanes] = value
+                    back_x[h, column, j - 1, later, lanes] = value[later].astype(BF16)
+        along(at_near, lambda side: x_back(h, side, 1).start())
+        for side in range(2):
+            for i in (1, 2):
+                for lanes, value in key_terms(i, 3 * side):
+                    back_z[h, side, SEAT[i], first, lanes] = value[first].astype(BF16)
+                    keep_z[h, side, i - 1, :, lanes] = value[later]
+        along(have_z, lambda side: z_back(h, side, 1, 0).start())
+        for i in (1, 2):
             for j in (1, 2):
                 for lanes, value in key_terms(i, j):
                     keep[h, i, j - 1, :, lanes] = value
-        return carry
-
-    def turn_x(h):
-        along(came_z, lambda side: z_back(h, side, 0).wait_recv())
-        for side in range(2):
-            for j in range(2):
-                both = keep[h, 3 * side, j] + from_z[h, j, side].astype(F32)
-                back_x[h, side, j] = both.astype(BF16)
-        along(have_x, lambda side: x_back(h, side).start())
-
-    def heads(h, carry):
-        attend(h, 0)
-
-        @pl.when(h == 0)
-        def _():
-            pass_corners(GROUP_HEADS - 1)
-
-        @pl.when(h > 0)
-        def _():
-            turn_x(h - 1)
-
-        return carry
-
-    lax.fori_loop(0, GROUP_HEADS, heads, 0)
-    turn_x(GROUP_HEADS - 1)
-
-    def finish(h, carry):
-        along(came_z, lambda side: z_back(h, side, 1).wait_recv())
-        along(came_x, lambda side: x_back(h, side).wait_recv())
-        for b in range(4):
-            i, j = b // 2, b % 2
-            whole = keep[h, 1 + i, j] + from_z[h, j, 2 + i].astype(F32)
-            low = (whole + from_x[h, i, j].astype(F32)).astype(BF16)
-            stage[h, b, 2] = low[:, :HEAD_DIM]
-            stage[h, b, 3] = low[:, HEAD_DIM:]
-        hand_out(1, h)
-        return carry
-
-    lax.fori_loop(0, GROUP_HEADS, finish, 0)
-
-    for a in range(3):
-        pair_copy(a).wait_send()
+        pl.when(h == 0)(lambda: pass_corners(2))
+        pl.when(h > 0)(lambda: finish(h - 1))
+        return carry
+
+    lax.fori_loop(0, GROUP_HEADS, attend, 0)
+    turn(GROUP_HEADS - 1)
+    finish(GROUP_HEADS - 1)
+
     for n in range(3):
         grad_copy(n).wait_send()
 
     def sent(h, carry):
+        for n in range(6):
+            pair_copy(h, n).wait_send()
         many = pl.ds(0, 16 * (chips - 1))
         pltpu.make_async_copy(recv.at[h, many], recv.at[h, many], all_send_sem.at[h]).wait()
         along(have_x, lambda side: x_side(h, side).wait_send())
         along(have_z, lambda side: z_side(h, side).wait_send())
-        corners(have_z, lambda column, side: corner(h, column, side).wait_send())
-        for kind in range(2):
-            along(have_z, lambda side: z_back(h, side, kind).wait_send())
-        along(have_x, lambda side: x_back(h, side).wait_send())
+        corners(have_z, lambda column, side: corner(h, column, side, 0).wait_send())
+        corners(have_z, lambda column, side: corner(h, column, side, 1).wait_send(), far_x)
+        corners(have_z, lambda column, side: cross(h, column, side).wait_send(), near_x)
+        for kind, part in ((0, 0), (1, 0), (1, 1)):
+            along(have_z, lambda side: z_back(h, side, kind, part).wait_send())
+        corners(have_z, lambda column, side: z_back_far(h, column, side).wait_send(), far_x)
+        corners(have_z, lambda column, side: x_cross(h, column, side).wait_send(), near_x)
+        for part in range(2):
+            along(have_x, lambda side: x_back(h, side, part).wait_send())
         return carry
 
     lax.fori_loop(0, GROUP_HEADS, sent, 0)
@@ -571,16 +661,19 @@
             pltpu.VMEM((4, d, tok), BF16),
             pltpu.VMEM((4, d, tok), BF16),
             pltpu.VMEM((gh, 4, 2, tok, 2 * d), F32),
+            pltpu.VMEM((gh, 2, 2, tok // 2, 2 * d), F32),
             pltpu.VMEM((gh, 2, 4, tok, 2 * d), BF16),
             pltpu.VMEM((gh, 2, 4, tok, 2 * d), BF16),
             pltpu.VMEM((gh, 2, 2, tok, 2 * d), BF16),
             pltpu.VMEM((gh, 2, 2, tok, 2 * d), BF16),
+            pltpu.VMEM((gh, 2, 2, tok // 2, 2 * d), BF16),
+            pltpu.VMEM((gh, 2, 2, tok // 2, 2 * d), BF16),
             pltpu.VMEM((gh, 4, 4, tok, d), BF16),
-            dma((3,)), dma((3,)), dma((3,)),
+            dma((gh, 6)), dma((gh, 6)), dma((gh, 6)),
             dma, dma((3,)), dma((3,)),
             dma((gh,)), dma((gh,)), dma((gh,)),
-            dma((gh, 4)), dma((gh, 4)), dma((gh, 4)), dma((gh, 4)),
-            dma((gh, 4)), dma((gh, 4)), dma((gh, 2)), dma((gh, 2)),
+            dma((gh, 4)), dma((gh, 4)), dma((gh, 8)), dma((gh, 8)), dma((gh, 4)),
+            dma((gh, 10)), dma((gh, 10)), dma((gh, 4)), dma((gh, 4)), dma((gh, 4)), dma((gh, 4)),
             dma((2,)), dma((2,)), dma((2,)),
         ],
         compiler_params=pltpu.CompilerParams(

time: 141 us -> 138 us (0.979); the launches traced: 141 us -> 136 us
  Pallas kernels: 139 us -> 134 us
    pallas_call x1, Pallas kernels: 136 us -> 131 us  [shards(): pl.pallas_call(functools.partial(kernel, nt, nh, cols), out_shape=jax.Sha...]
where the time goes in v5:
time: 138 us; the launch traced here: 136 us
  Pallas kernels  134 us (97%)
  local copies, waits for them, and re-layouts  1.6 us (1%)
    pallas_call x1, Pallas kernels, shards(): pl.pallas_call(functools.partial(kernel, nt, nh, cols), out_shape=jax.Sha...  131 us
    pallas_call x1, Pallas kernels, shards(): pl.pallas_call(deal, out_shape=[low] * 4, in_specs=[hbm], out_specs=[hbm]...  2.86 us

profile of v5, /device:TPU:33, one launch (start us, length us, event | category | flops | bytes accessed | tf_op | source)
XLA Modules:
  0.0 136.4 jit_solution(9545782034964778987)
XLA Ops:
  0.6 1.6 %reshape.26.order_ref = s32[128,256]{1,0:T(8,128)} reshape(s32[32768]{0:T(1024)} %param.8) | data formatting | bytes 262144 | tf_op jit(solution)/shard_map/reshape | solution.py:687
  2.2 131.1 %shard_map.84.in_ref = bf16[4,256,1536]{2,1,0:T(8,128)(2,1)} custom-call(bf16[256,1536]{1,0:T(8,128)(2,1)} %q_ref.1, bf16[256,1536]{1,0:T(8,128)(2,1)} %k_ref.1, bf16[256,1536]{1,0:T(8,128)(2,1)} %v_ref.1, s32[128,256]{1,0:T(8,128)} %reshape.26.order_ref, bf16[256,1536]{1,0:T(8,128)(2,1)} %bitcast.5), custom_call_target="tpu_custom_call" | custom-call | flops 10871635968 | bytes 6291456 | tf_op jit(solution)/shard_map/pallas_call | solution.py:642
  133.4 2.9 %shard_map.85 = (bf16[256,1536]{1,0:T(8,128)(2,1)}, bf16[256,1536]{1,0:T(8,128)(2,1)}, bf16[256,1536]{1,0:T(8,128)(2,1)}, bf16[256,1536]{1,0:T(8,128)(2,1)}) custom-call(bf16[4,256,1536]{2,1,0:T(8,128)(2,1)} %shard_map.84.in_ref), custom_call_target="tpu_custom_call" | custom-call | tf_op jit(solution)/shard_map/pallas_call | solution.py:688

commit v6 on v5

--- a/solution.py
+++ b/solution.py
@@ -184,11 +184,18 @@
         inside = ((frame % TILE_FRAMES) * TILE_ROWS + row % TILE_ROWS) * cols + t % cols
         return frame_block, row_block, inside
 
-    order = order_ref[...]
+    pieces = tok // order_ref.shape[1]
+
+    def source_rows(first, count, step):
+        return jnp.concatenate(
+            [order_ref[pl.ds(first * pieces + n, count, step), :] for n in range(pieces)], axis=1
+        )
+
+    order = source_rows(0, nt * nh, pieces)
     order_t = order.T
     for cc in range(2):
         source = kk * 2 * nh + cc * nh + ha
-        line = order_ref[pl.ds(source, 1), :]
+        line = source_rows(source, 1, 1)
         column = jnp.sum(
             jnp.where(iota(order_t.shape, 1) == source, order_t, 0), axis=1, keepdims=True
         )
@@ -684,7 +691,7 @@
             bytes_accessed=16 * tok * channels,
             transcendentals=4 * gh * 9 * tok * tok,
         ),
-    )(query_seq, key_seq, value_seq, tile_order.reshape(nt * nh, tok), grad_output.reshape(tok, channels))
+    )(query_seq, key_seq, value_seq, tile_order.reshape(-1, min(tok, 128)), grad_output.reshape(tok, channels))
     outs = pl.pallas_call(
         deal,
         out_shape=[low] * 4,

time: 138 us -> 136 us (0.986)
  local copies, waits for them, and re-layouts: 1.6 us -> 0 us
    reshape x1 -> x0, local copies, waits for them, and re-layouts: 1.6 us -> none  [shards(): tile_order.reshape(nt * nh, tok)]
where the time goes in v6:
time: 136 us; the launch traced here: 135 us
  Pallas kernels  134 us (99%)
    pallas_call x1, Pallas kernels, shards(): pl.pallas_call(functools.partial(kernel, nt, nh, cols), out_shape=jax.Sha...  131 us
    pallas_call x1, Pallas kernels, shards(): pl.pallas_call(deal, out_shape=[low] * 4, in_specs=[hbm], out_specs=[hbm]...  2.86 us

profile of v6, /device:TPU:33, one launch (start us, length us, event | category | flops | bytes accessed | tf_op | source)
XLA Modules:
  0.0 134.9 jit_solution(6876179786390622290)
XLA Ops:
  0.6 131.2 %shard_map.84.in_ref = bf16[4,256,1536]{2,1,0:T(8,128)(2,1)} custom-call(bf16[256,1536]{1,0:T(8,128)(2,1)} %q_ref.1, bf16[256,1536]{1,0:T(8,128)(2,1)} %k_ref.1, bf16[256,1536]{1,0:T(8,128)(2,1)} %v_ref.1, s32[256,128]{1,0:T(8,128)} %bitcast.11, bf16[256,1536]{1,0:T(8,128)(2,1)} %bitcast.6), custom_call_target="tpu_custom_call" | custom-call | flops 10871635968 | bytes 6291456 | tf_op jit(solution)/shard_map/pallas_call | solution.py:649
  131.9 2.9 %shard_map.85 = (bf16[256,1536]{1,0:T(8,128)(2,1)}, bf16[256,1536]{1,0:T(8,128)(2,1)}, bf16[256,1536]{1,0:T(8,128)(2,1)}, bf16[256,1536]{1,0:T(8,128)(2,1)}) custom-call(bf16[4,256,1536]{2,1,0:T(8,128)(2,1)} %shard_map.84.in_ref), custom_call_target="tpu_custom_call" | custom-call | tf_op jit(solution)/shard_map/pallas_call | solution.py:695

commit v7 on v6

--- a/solution.py
+++ b/solution.py
@@ -477,13 +477,17 @@
         for part in range(2):
             along(came_z, lambda side: z_back(h, side, 1, part).wait_recv())
             along(came_x, lambda side: x_back(h, side, part).wait_recv())
-        for b in range(4):
-            i, j = b // 2, b % 2
+        for n in (1, 2, 0, None):
+            i, j = (core, half) if n is None else others[n]
+            b = 2 * i + j
             whole = keep[h, 1 + i, j] + from_z[h, j, 2 + i].astype(F32)
             low = (whole + from_x[h, i, j].astype(F32)).astype(BF16)
             stage[h, b, 2] = low[:, :HEAD_DIM]
             stage[h, b, 3] = low[:, HEAD_DIM:]
-        hand_out(1, h)
+            if n is None:
+                out_own(1, h).start()
+            else:
+                out_copy(1, h, n).start()
 
     def attend(h, carry):
         for part in range(2):

time: 136 us -> 136 us (level)
  no operation moved by 1% of the time
where the time goes in v7:
time: 136 us; the launch traced here: 135 us
  Pallas kernels  134 us (99%)
    pallas_call x1, Pallas kernels, shards(): pl.pallas_call(functools.partial(kernel, nt, nh, cols), out_shape=jax.Sha...  131 us
    pallas_call x1, Pallas kernels, shards(): pl.pallas_call(deal, out_shape=[low] * 4, in_specs=[hbm], out_specs=[hbm]...  2.86 us

profile of v7, /device:TPU:33, one launch (start us, length us, event | category | flops | bytes accessed | tf_op | source)
XLA Modules:
  0.0 134.8 jit_solution(14963409539625513407)
XLA Ops:
  0.6 131.1 %shard_map.84.in_ref = bf16[4,256,1536]{2,1,0:T(8,128)(2,1)} custom-call(bf16[256,1536]{1,0:T(8,128)(2,1)} %q_ref.1, bf16[256,1536]{1,0:T(8,128)(2,1)} %k_ref.1, bf16[256,1536]{1,0:T(8,128)(2,1)} %v_ref.1, s32[256,128]{1,0:T(8,128)} %bitcast.11, bf16[256,1536]{1,0:T(8,128)(2,1)} %bitcast.6), custom_call_target="tpu_custom_call" | custom-call | flops 10871635968 | bytes 6291456 | tf_op jit(solution)/shard_map/pallas_call | solution.py:653
  131.7 2.9 %shard_map.85 = (bf16[256,1536]{1,0:T(8,128)(2,1)}, bf16[256,1536]{1,0:T(8,128)(2,1)}, bf16[256,1536]{1,0:T(8,128)(2,1)}, bf16[256,1536]{1,0:T(8,128)(2,1)}) custom-call(bf16[4,256,1536]{2,1,0:T(8,128)(2,1)} %shard_map.84.in_ref), custom_call_target="tpu_custom_call" | custom-call | tf_op jit(solution)/shard_map/pallas_call | solution.py:699
